TPU v7x, 32 devices: a whole 2x2x4 slice. The times are simulated.
32 devices in a mesh: rep: 8 (over z, x), fsdp: 4 (over y, core).
Axes of the slice: x: 2, y: 2, z: 4, core: 2. Of those that a mesh axis runs over, the one named last changes fastest.
Arguments:
- tokens: bfloat16 [4096, 768], P(('rep', 'fsdp')), may hold values from -6 to 6
- expert_ids: int32 [4096, 1], P(('rep', 'fsdp')), may hold values from 0 to 1; in each aligned block of 128 rows (0 to 127, 128 to 255, ...) at most 68 rows name the same one
- seq_lengths: int32 [8, 2], P('rep'), may hold values from 1 to 432, 496 in all within a row
- rel_buckets: int32 [1023], replicated, may hold values from 0 to 31, as said below
- attn_qkv: bfloat16 [3, 768, 768], P(None, 'fsdp'), may hold values from -0.21875 to 0.21875
- attn_out: bfloat16 [768, 768], P('fsdp'), may hold values from -4 to 4
- norm_gains: bfloat16 [2, 768], P(None, 'fsdp'), may hold values from 0.099609375 to 1.8984375
- bias_table: bfloat16 [32, 12], P('fsdp'), may hold values from -4 to 4
- router: bfloat16 [768, 2], P('fsdp'), may hold values from -0.21875 to 0.21875
- w_in: bfloat16 [2, 768, 3072], P(None, None, 'fsdp'), may hold values from -0.21875 to 0.21875
- w_out: bfloat16 [2, 3072, 768], P(None, 'fsdp'), may hold values from -0.21875 to 0.21875
- cotangent: bfloat16 [4096, 768], P(('rep', 'fsdp')), may hold values from -6 to 6
Outputs:
- mixed: bfloat16 [4096, 768], P(('rep', 'fsdp'))
- grad_tokens: float32 [4096, 768], P(('rep', 'fsdp'))
- grad_qkv: float32 [3, 768, 768], P(None, ('rep', 'fsdp'))
- grad_out: float32 [768, 768], P(('rep', 'fsdp'))
- grad_gains: float32 [2, 768], P(None, 'fsdp')
- grad_table: float32 [32, 12], P('fsdp')
- grad_router: float32 [768, 2], P('fsdp')
- grad_w_in: float32 [2, 768, 3072], P(None, 'rep', 'fsdp')
- grad_w_out: float32 [2, 3072, 768], P(None, ('rep', 'fsdp'))
Inputs may be any that keep to these rules, and one draw needn't show every extreme that they name: `expert_ids`: each row names the expert of its token; the 128 rows of one device name one expert at most 68 times. `seq_lengths`: row g lists in order the lengths of the sequences packed into the 512 places of group g; they sum to 496, the remaining places are padding that attends only to padding, and none is longer than 432. `rel_buckets`: entry 511 + r is the bucket of the relative position r = key place minus query place.
All inputs are finite; a program needn't handle non-finite values.
Results may differ from a plain program's by a relative error of at most 0.015.
Values may be sent and summed in bfloat16 or wider, within the bound.
A program may use at most 192 MiB of HBM per device.

v0:
```python
from functools import partial

import jax
import jax.numpy as jnp
from jax import lax
from jax.sharding import PartitionSpec as P

D = 768
H = 12
HD = 64
FF = 3072
NB = 32
EXPERTS = 2
CAP = 68


NORM_EPSILON = 1e-06
SCORE_SCALE = 0.125
MASKED_SCORE = -1000000000.0
HIGHEST_PRECISION = lax.Precision.HIGHEST


def norm_rows(values, weights):
    return (
        values
        * lax.rsqrt(jnp.mean(values * values, axis=-1, keepdims=True) + NORM_EPSILON)
        * weights
    )


def product(left, right):
    return jnp.dot(left, right, preferred_element_type=jnp.float32)


def product_tn(left, right):
    return lax.dot_general(
        left, right, (((0,), (0,)), ((), ())), preferred_element_type=jnp.float32
    )


def product_nt(left, right):
    return lax.dot_general(
        left, right, (((1,), (1,)), ((), ())), preferred_element_type=jnp.float32
    )


def owner_order(positions, total, fsdp_count, rep_count):
    block_size = total // (rep_count * fsdp_count)
    share_size = total // fsdp_count
    owner_fsdp = positions // share_size
    within = positions % share_size
    owner_rep = within // block_size
    offset = within % block_size
    return (owner_rep * fsdp_count + owner_fsdp) * block_size + offset


def bucket_codes(rel_buckets, first_query, row_count, key_count, group_rows):
    span_length = row_count + key_count - 1
    picked = lax.dynamic_slice_in_dim(
        rel_buckets, group_rows - row_count - first_query, span_length
    )
    return (picked[:, None] == jnp.arange(NB, dtype=jnp.int32)[None, :]).astype(jnp.bfloat16)


def expand_bias(table_full, codes, row_count, key_count):
    along = lax.dot_general(
        table_full, codes, (((0,), (1,)), ((), ())), preferred_element_type=jnp.float32
    )
    span_length = along.shape[1]
    turned = jnp.concatenate([along[:, row_count - 1 :], along[:, : row_count - 1]], axis=1)
    tiled = jnp.tile(turned, (1, row_count))[:, : row_count * (span_length - 1)]
    return tiled.reshape(along.shape[0], row_count, span_length - 1)[:, :, :key_count]


def table_grad(grad_scores, codes, row_count, key_count):
    head_count = grad_scores.shape[0]
    span_length = codes.shape[0]
    widened = jnp.pad(
        grad_scores.astype(jnp.float32), ((0, 0), (0, 0), (0, span_length - 1 - key_count))
    )
    flat = jnp.pad(
        widened.reshape(head_count, row_count * (span_length - 1)), ((0, 0), (0, row_count))
    )
    turned = jnp.sum(flat.reshape(head_count, row_count, span_length), axis=1)
    cut_point = span_length - row_count + 1
    along = jnp.concatenate([turned[:, cut_point:], turned[:, :cut_point]], axis=1)
    return lax.dot_general(
        codes.astype(jnp.float32),
        along,
        (((0,), (1,)), ((), ())),
        precision=HIGHEST_PRECISION,
        preferred_element_type=jnp.float32,
    )


def attention_probs(queries, keys_all, bias, same_seq):
    raw_scores = (
        jnp.einsum("qhd,khd->hqk", queries, keys_all, preferred_element_type=jnp.float32)
        * SCORE_SCALE
        + bias
    )
    return jax.nn.softmax(jnp.where(same_seq[None], raw_scores, MASKED_SCORE), axis=-1)


def local(
    tokens,
    expert_ids,
    seq_lengths,
    rel_buckets,
    attn_qkv,
    attn_out,
    norm_gains,
    bias_table,
    router,
    w_in,
    w_out,
    cotangent,
):
    row_count = tokens.shape[0]
    fsdp_count = lax.axis_size("fsdp")
    rep_count = lax.axis_size("rep")
    group_rows = row_count * fsdp_count
    first_query = lax.axis_index("fsdp") * row_count
    places = jnp.arange(group_rows, dtype=jnp.int32)
    seq_ends = jnp.cumsum(seq_lengths[0])
    seq_all = jnp.sum((places[:, None] >= seq_ends[None, :]).astype(jnp.int32), axis=1)
    seq_own = lax.dynamic_slice_in_dim(seq_all, first_query, row_count)
    same_seq = seq_own[:, None] == seq_all[None, :]
    codes = bucket_codes(rel_buckets, first_query, row_count, group_rows, group_rows)
    head_shape = (-1, H, HD)
    qkv_full, out_full, gains_full, table_full, router_full = (
        lax.all_gather(attn_qkv, "fsdp", axis=1, tiled=True),
        lax.all_gather(attn_out, "fsdp", axis=0, tiled=True),
        lax.all_gather(norm_gains, "fsdp", axis=1, tiled=True),
        lax.all_gather(bias_table, "fsdp", axis=0, tiled=True),
        lax.all_gather(router, "fsdp", axis=0, tiled=True),
    )
    w_in_full, w_out_full = (
        lax.all_gather(w_in, "fsdp", axis=2, tiled=True),
        lax.all_gather(w_out, "fsdp", axis=1, tiled=True),
    )
    inputs = tokens.astype(jnp.float32)
    gain_one = gains_full[0].astype(jnp.float32)
    normed = norm_rows(inputs, gain_one).astype(jnp.bfloat16)
    queries = product(normed, qkv_full[0]).astype(jnp.bfloat16)
    keys_own = product(normed, qkv_full[1]).astype(jnp.bfloat16)
    values_own = product(normed, qkv_full[2]).astype(jnp.bfloat16)
    keys_all, values_all = (
        lax.all_gather(keys_own, "fsdp", axis=0, tiled=True),
        lax.all_gather(values_own, "fsdp", axis=0, tiled=True),
    )
    bias = expand_bias(table_full, codes, row_count, group_rows)
    probs = attention_probs(
        queries.reshape(head_shape), keys_all.reshape(head_shape), bias, same_seq
    )
    attended = (
        jnp.einsum(
            "hqk,khd->qhd",
            probs.astype(jnp.bfloat16),
            values_all.reshape(head_shape),
            preferred_element_type=jnp.float32,
        )
        .reshape(row_count, D)
        .astype(jnp.bfloat16)
    )
    hidden = inputs + product(attended, out_full)
    gain_two = gains_full[1].astype(jnp.float32)
    hidden_normed = norm_rows(hidden, gain_two).astype(jnp.bfloat16)
    logits = product(hidden_normed, router_full)
    chosen = (expert_ids == jnp.arange(EXPERTS, dtype=jnp.int32)[None, :]).astype(jnp.int32)
    chosen_float = chosen.astype(jnp.float32)

    def gate_of(values):
        return jnp.sum(jax.nn.softmax(values, axis=-1) * chosen_float, axis=1, keepdims=True)

    gating = gate_of(logits)
    earlier = jnp.cumsum(chosen, axis=0) - chosen
    slot_index = jnp.sum(earlier * chosen, axis=1)
    target = expert_ids[:, 0] * CAP + slot_index
    source = (
        jnp.zeros((EXPERTS * CAP,), jnp.int32)
        .at[target]
        .set(jnp.arange(row_count, dtype=jnp.int32))
    )
    filled = jnp.zeros((EXPERTS * CAP, 1), jnp.bfloat16).at[target].set(1.0)
    tiles = hidden_normed[source].reshape(EXPERTS, CAP, D)
    expert_in = jnp.einsum("ecd,edf->ecf", tiles, w_in_full, preferred_element_type=jnp.float32)
    activation = jax.nn.gelu(expert_in, approximate=True).astype(jnp.bfloat16)
    expert_out = jnp.einsum(
        "ecf,efd->ecd", activation, w_out_full, preferred_element_type=jnp.float32
    )
    routed = expert_out.reshape(EXPERTS * CAP, D)[target]
    mixed = (hidden + gating * routed).astype(jnp.bfloat16)
    (
        qkv_full,
        out_full,
        gains_full,
        table_full,
        router_full,
        w_in_full,
        w_out_full,
        keys_all,
        values_all,
    ) = (
        lax.all_gather(attn_qkv, "fsdp", axis=1, tiled=True),
        lax.all_gather(attn_out, "fsdp", axis=0, tiled=True),
        lax.all_gather(norm_gains, "fsdp", axis=1, tiled=True),
        lax.all_gather(bias_table, "fsdp", axis=0, tiled=True),
        lax.all_gather(router, "fsdp", axis=0, tiled=True),
        lax.all_gather(w_in, "fsdp", axis=2, tiled=True),
        lax.all_gather(w_out, "fsdp", axis=1, tiled=True),
        lax.all_gather(keys_own, "fsdp", axis=0, tiled=True),
        lax.all_gather(values_own, "fsdp", axis=0, tiled=True),
    )
    gain_one = gains_full[0].astype(jnp.float32)
    gain_two = gains_full[1].astype(jnp.float32)
    grad_mixed = cotangent.astype(jnp.float32)
    grad_routed = (gating * grad_mixed).astype(jnp.bfloat16)
    grad_gate = jnp.sum(grad_mixed * routed, axis=1, keepdims=True)
    grad_tiles = (grad_routed[source] * filled).reshape(EXPERTS, CAP, D)
    grad_act = jnp.einsum(
        "ecd,efd->ecf", grad_tiles, w_out_full, preferred_element_type=jnp.float32
    )
    gelu_pull = jax.vjp(partial(jax.nn.gelu, approximate=True), expert_in)[1]
    grad_in = gelu_pull(grad_act)[0].astype(jnp.bfloat16)
    grad_normed_two = jnp.einsum(
        "ecf,edf->ecd", grad_in, w_in_full, preferred_element_type=jnp.float32
    ).reshape(EXPERTS * CAP, D)[target]
    grad_logits = jax.vjp(gate_of, logits)[1](grad_gate)[0]
    router_wide = router_full.astype(jnp.float32)
    grad_normed_two = grad_normed_two + lax.dot_general(
        grad_logits,
        router_wide,
        (((1,), (1,)), ((), ())),
        precision=HIGHEST_PRECISION,
        preferred_element_type=jnp.float32,
    )
    grad_router = lax.dot_general(
        hidden_normed.astype(jnp.float32),
        grad_logits,
        (((0,), (0,)), ((), ())),
        precision=HIGHEST_PRECISION,
        preferred_element_type=jnp.float32,
    )
    grad_hidden_part, grad_gain_two = jax.vjp(norm_rows, hidden, gain_two)[1](grad_normed_two)
    grad_hidden = grad_mixed + grad_hidden_part
    grad_branch = grad_hidden.astype(jnp.bfloat16)
    grad_attended = product_nt(grad_branch, out_full).astype(jnp.bfloat16)
    queries_split = queries.reshape(head_shape)
    keys_split = keys_all.reshape(head_shape)
    values_split = values_all.reshape(head_shape)
    grad_split = grad_attended.reshape(head_shape)
    bias = expand_bias(table_full, codes, row_count, group_rows)
    probs = attention_probs(queries_split, keys_split, bias, same_seq)
    grad_probs = jnp.einsum(
        "qhd,khd->hqk", grad_split, values_split, preferred_element_type=jnp.float32
    )
    grad_scores = (
        probs * (grad_probs - jnp.sum(probs * grad_probs, axis=-1, keepdims=True))
    ).astype(jnp.bfloat16)
    grad_queries = (
        (
            jnp.einsum("hqk,khd->qhd", grad_scores, keys_split, preferred_element_type=jnp.float32)
            * SCORE_SCALE
        )
        .reshape(row_count, D)
        .astype(jnp.bfloat16)
    )
    key_terms = (
        jnp.einsum("hqk,qhd->khd", grad_scores, queries_split, preferred_element_type=jnp.float32)
        * SCORE_SCALE
    ).reshape(group_rows, D)
    value_terms = jnp.einsum(
        "hqk,qhd->khd", probs.astype(jnp.bfloat16), grad_split, preferred_element_type=jnp.float32
    ).reshape(group_rows, D)
    grad_keys, grad_values = (
        lax.psum_scatter(
            key_terms.astype(jnp.bfloat16), "fsdp", scatter_dimension=0, tiled=True
        ).astype(jnp.float32),
        lax.psum_scatter(
            value_terms.astype(jnp.bfloat16), "fsdp", scatter_dimension=0, tiled=True
        ).astype(jnp.float32),
    )
    grad_keys = grad_keys.astype(jnp.bfloat16)
    grad_values = grad_values.astype(jnp.bfloat16)
    grad_table = table_grad(grad_scores, codes, row_count, group_rows)
    grad_normed = (
        product_nt(grad_queries, qkv_full[0])
        + product_nt(grad_keys, qkv_full[1])
        + product_nt(grad_values, qkv_full[2])
    )
    grad_input_part, grad_gain_one = jax.vjp(norm_rows, inputs, gain_one)[1](grad_normed)
    grad_tokens = grad_hidden + grad_input_part
    grad_gains = jnp.stack([grad_gain_one, grad_gain_two])
    grad_stack = jnp.concatenate([grad_queries, grad_keys, grad_values], axis=1)
    picked = owner_order(
        jnp.arange(D // fsdp_count * lax.axis_size("fsdp"), dtype=jnp.int32),
        D,
        fsdp_count,
        rep_count,
    )
    qkv_share = lax.psum_scatter(
        product_tn(jnp.take(normed, picked, axis=1), grad_stack).astype(jnp.bfloat16),
        "fsdp",
        scatter_dimension=0,
        tiled=True,
    ).astype(jnp.float32)
    picked = owner_order(
        jnp.arange(D // fsdp_count * lax.axis_size("fsdp"), dtype=jnp.int32),
        D,
        fsdp_count,
        rep_count,
    )
    out_share = lax.psum_scatter(
        product_tn(jnp.take(attended, picked, axis=1), grad_branch).astype(jnp.bfloat16),
        "fsdp",
        scatter_dimension=0,
        tiled=True,
    ).astype(jnp.float32)
    in_share = lax.psum_scatter(
        jnp.einsum("ecd,ecf->fed", tiles, grad_in, preferred_element_type=jnp.float32).astype(
            jnp.bfloat16
        ),
        "fsdp",
        scatter_dimension=0,
        tiled=True,
    ).astype(jnp.float32)
    picked = owner_order(
        jnp.arange(FF // fsdp_count * lax.axis_size("fsdp"), dtype=jnp.int32),
        FF,
        fsdp_count,
        rep_count,
    )
    outer_share = lax.psum_scatter(
        jnp.einsum(
            "ecf,ecd->fed",
            jnp.take(activation, picked, axis=2),
            grad_tiles,
            preferred_element_type=jnp.float32,
        ).astype(jnp.bfloat16),
        "fsdp",
        scatter_dimension=0,
        tiled=True,
    ).astype(jnp.float32)
    grad_gains, grad_table, grad_router = (
        lax.psum_scatter(grad_gains, "fsdp", scatter_dimension=1, tiled=True),
        lax.psum_scatter(grad_table, "fsdp", scatter_dimension=0, tiled=True),
        lax.psum_scatter(grad_router, "fsdp", scatter_dimension=0, tiled=True),
    )
    qkv_share, out_share, in_share, outer_share = (
        lax.psum_scatter(qkv_share, "rep", scatter_dimension=0, tiled=True),
        lax.psum_scatter(out_share, "rep", scatter_dimension=0, tiled=True),
        lax.psum_scatter(in_share, "rep", scatter_dimension=2, tiled=True),
        lax.psum_scatter(outer_share, "rep", scatter_dimension=0, tiled=True),
    )
    grad_gains, grad_table, grad_router = lax.psum((grad_gains, grad_table, grad_router), "rep")
    grad_qkv = jnp.transpose(qkv_share.reshape(qkv_share.shape[0], 3, D), (1, 0, 2))
    grad_w_in = jnp.transpose(in_share, (1, 2, 0))
    grad_w_out = jnp.transpose(outer_share, (1, 0, 2))
    return (
        mixed,
        grad_tokens,
        grad_qkv,
        out_share,
        grad_gains,
        grad_table,
        grad_router,
        grad_w_in,
        grad_w_out,
    )


def solution(mesh):
    return jax.shard_map(
        local,
        mesh=mesh,
        in_specs=(
            P(("rep", "fsdp"), None),
            P(("rep", "fsdp"), None),
            P("rep", None),
            P(),
            P(None, "fsdp", None),
            P("fsdp", None),
            P(None, "fsdp"),
            P("fsdp", None),
            P("fsdp", None),
            P(None, None, "fsdp"),
            P(None, "fsdp", None),
            P(("rep", "fsdp"), None),
        ),
        out_specs=(
            P(("rep", "fsdp"), None),
            P(("rep", "fsdp"), None),
            P(None, ("rep", "fsdp"), None),
            P(("rep", "fsdp"), None),
            P(None, "fsdp"),
            P("fsdp", None),
            P("fsdp", None),
            P(None, "rep", "fsdp"),
            P(None, ("rep", "fsdp"), None),
        ),
        check_vma=False,
    )
```

profile of v0, /device:TPU:2, one launch (start us, length us, event | category | flops | bytes accessed | tf_op | source)
XLA Modules:
  0.0 1009.8 jit_solution(1753004816140002448)
XLA Ops:
  10.2 5.2 all_gather.40
  31.8 6.1 tile.5
  37.9 5.1 slice.73
  43.0 7.3 reshape.310
  55.1 9.2 all_gather.38
  66.5 9.0 all_gather.39
  81.2 5.8 convolution_convert_fusion.4
  90.8 36.1 %all-gather.11.cloned.1.call-done = bf16[2,768,3072]{2,1,0:T(8,128)(2,1)} async-done(((bf16[2,768,768]{2,1,0:T(8,128)(2,1)}), bf16[2,768,3072]{2,1,0:T(8,128)(2,1)}) %all-gather.11.cloned.1.call-update) | async-done | bytes 9437200 | tf_op jit(solution)/shard_map/all_gather | solution.py:139
  126.9 7.0 multiply_convert_fusion.1
  133.9 59.4 %all-gather.13.cloned.1.call-done = bf16[2,3072,768]{2,1,0:T(8,128)(2,1)} async-done(((bf16[2,768,768]{2,1,0:T(8,128)(2,1)}), bf16[2,3072,768]{2,1,0:T(8,128)(2,1)}) %all-gather.13.cloned.1.call-update) | async-done | bytes 9437200 | tf_op jit(solution)/shard_map/all_gather | solution.py:140
  193.3 5.3 fusion.115
  204.3 7.5 fusion.8
  224.7 6.7 convolution_convert_fusion.2
  247.8 9.4 reduce-scatter.33.cloned.1.call-done
  258.3 24.8 %reduce-scatter.31.cloned.1.call-done = bf16[128,768]{1,0:T(8,128)(2,1)} async-done(((bf16[512,768]{1,0:T(8,128)(2,1)}), bf16[128,768]{1,0:T(8,128)(2,1)}) %reduce-scatter.31.cloned.1.call-update) | async-done | bytes 196624
  290.4 21.9 %gather_fusion.4 = bf16[3072,2,68]{2,1,0:T(2,128)(2,1)} fusion(bf16[2,68,3072]{1,0,2:T(2,128)(2,1)} %copy.75, s32[3072]{0:T(1024)S(1)} %broadcast_clamp_fusion), kind=kCustom, calls=%fused_computation.6 | custom fusion | bytes 1683456 | tf_op jit(solution)/shard_map/jit(_take)/gather | solution.py:337
  312.4 12.1 %fusion.10 = bf16[2,68,3072]{1,0,2:T(2,128)(2,1)S(1)} fusion(bf16[3072,2,68]{2,1,0:T(2,128)(2,1)} %gather_fusion.4, pred[3072]{0:T(1024)(128)(4,1)S(1)} %compare_and_fusion), kind=kLoop, calls=%fused_computation.33 | loop fusion | flops 417792 | bytes 1674240 | tf_op jit(solution)/shard_map/jit(_take)/select_n | solution.py:337
  324.5 5.2 convert_bitcast_fusion
  330.8 5.1 convert_bitcast_fusion.1
  351.1 57.9 %reduce-scatter.29.cloned.1.call-done = bf16[768,2,768]{0,2,1:T(8,128)(2,1)} async-done(((bf16[3072,2,768]{0,2,1:T(8,128)(2,1)}), bf16[768,2,768]{0,2,1:T(8,128)(2,1)}) %reduce-scatter.29.cloned.1.call-update) | async-done | bytes 2359312 | tf_op jit(solution)/shard_map/reduce_scatter | solution.py:334
  409.0 7.2 copy.77
  416.2 74.1 %reduce-scatter.27.cloned.1.call-done = bf16[768,2,768]{2,0,1:T(8,128)(2,1)} async-done(((bf16[3072,2,768]{2,0,1:T(8,128)(2,1)}), bf16[768,2,768]{2,0,1:T(8,128)(2,1)}) %reduce-scatter.27.cloned.1.call-update) | async-done | bytes 2359312 | tf_op jit(solution)/shard_map/reduce_scatter | solution.py:320
  490.2 7.2 copy.74
  503.5 5.3 reshape.318
  508.8 9.8 reduce-scatter.23.cloned.1.call-done
  523.0 6.9 reshape.324
  532.8 10.6 %all-reduce.2 = f32[32,12]{1,0:T(8,128)S(1)} all-reduce(f32[32,12]{1,0:T(8,128)S(1)} %fusion.41), channel_id=9, replica_groups=mesh['rep'=8,'fsdp'=4] {'fsdp'}, use_global_device_ids=true, to_apply=%region_29.31.clone | all-reduce | flops 384 | bytes 3072
  545.3 21.0 %reduce-scatter.35.cloned.1.call-done = f32[192,2]{1,0:T(8,128)} async-done(((f32[768,2]{1,0:T(8,128)}), f32[192,2]{1,0:T(8,128)}) %reduce-scatter.35.cloned.1.call-update) | async-done | bytes 1552
  567.3 18.6 %all-reduce.5 = (f32[2,192]{1,0:T(2,128)}, f32[8,12]{1,0:T(8,128)}, f32[192,2]{0,1:T(2,128)}) all-reduce(f32[2,192]{1,0:T(2,128)S(1)} %copy.86, f32[8,12]{1,0:T(8,128)S(1)} %constant_dynamic-slice_fusion, f32[192,2]{0,1:T(2,128)S(1)} %copy.88), channel_id=1, replica_groups=mesh['rep'=8,'fsdp'=4] {'rep'}, use_global_device_ids=true, to_apply=%region_27.29 | all-reduce | flops 864 | bytes 6912 | tf_op jit(solution)/shard_map/psum | solution.py:356
  585.9 49.2 %reduce-scatter.21.cloned.1.call-done = f32[24,2304]{1,0:T(8,128)} async-done(((f32[192,2304]{1,0:T(8,128)}), f32[24,2304]{1,0:T(8,128)}) %reduce-scatter.21.cloned.1.call-update) | async-done | bytes 221200 | tf_op jit(solution)/shard_map/reduce_scatter | solution.py:351
  636.9 301.2 %all-reduce.9.cloned.1.call-done = (f32[768,2,768]{0,1,2:T(2,128)}, f32[768,2,768]{2,1,0:T(2,128)}) async-done(((f32[768,2,768]{0,1,2:T(2,128)}, f32[768,2,768]{2,1,0:T(2,128)}), (f32[768,2,768]{0,1,2:T(2,128)}, f32[768,2,768]{2,1,0:T(2,128)})) %all-reduce.9.cloned.1.call-update) | async-done | bytes 9437200
  942.0 61.0 %reduce-scatter.25.cloned.1.call-done = f32[24,768]{1,0:T(8,128)} async-done(((f32[192,768]{1,0:T(8,128)}), f32[24,768]{1,0:T(8,128)}) %reduce-scatter.25.cloned.1.call-update) | async-done | bytes 73744 | tf_op jit(solution)/shard_map/reduce_scatter | solution.py:352
  (276 shorter events, 115.2 us)
Async XLA Ops:
  7.2 44.4 %all-gather.7.cloned.1.call-start = ((), (), s32[]{:S(2)}) async-start(), calls=%async_computation.10 | async-start | bytes 4423680 | tf_op jit(solution)/shard_map/all_gather | solution.py:132
  7.9 79.1 %all-gather.9.cloned.1.call-start = ((), (), s32[]{:S(2)}) async-start(), calls=%async_computation.11 | async-start | bytes 1474560 | tf_op jit(solution)/shard_map/all_gather | solution.py:133
  8.7 12.3 %copy-start.52 = (bf16[192,2]{0,1:T(2,128)(2,1)S(1)}, bf16[192,2]{0,1:T(2,128)(2,1)}, u32[]{:S(2)}) copy-start(bf16[192,2]{0,1:T(2,128)(2,1)} %param.22) | copy-start | bytes 2308
  8.7 17.5 %copy-start.28 = (s32[128,1]{0,1:T(1,128)S(1)}, s32[128,1]{0,1:T(1,128)}, u32[]{:S(2)}) copy-start(s32[128,1]{0,1:T(1,128)} %param.15) | copy-start | bytes 1540
  8.7 118.2 %all-gather.11.cloned.1.call-start = ((), (), s32[]{:S(2)}) async-start(), calls=%async_computation.12 | async-start | bytes 11796480 | tf_op jit(solution)/shard_map/all_gather | solution.py:139
  9.5 183.9 %all-gather.13.cloned.1.call-start = ((), (), s32[]{:S(2)}) async-start(), calls=%async_computation.13 | async-start | bytes 11796480 | tf_op jit(solution)/shard_map/all_gather | solution.py:140
  10.0 247.2 %reduce-scatter.33.cloned.1.call-start = ((), (), s32[]{:S(2)}) async-start(), calls=%async_computation.21 | async-start | bytes 983040
  51.1 38.5 %copy-start.27 = (s32[1024]{0:T(1024)}, s32[1024]{0:T(1024)S(1)}, u32[]{:S(2)}) copy-start(s32[1024]{0:T(1024)S(1)} %pad_clamp_fusion.2) | copy-start | bytes 12292
  51.3 13.0 %copy-start.53 = (f32[128]{0:T(128)}, f32[128]{0:T(128)S(1)}, u32[]{:S(2)}) copy-start(f32[128]{0:T(128)S(1)} %fusion.27) | copy-start | bytes 1540
  51.3 13.0 %copy-start.47 = (f32[128]{0:T(128)}, f32[128]{0:T(128)S(1)}, u32[]{:S(2)}) copy-start(f32[128]{0:T(128)S(1)} %fusion.106) | copy-start | bytes 1540
  51.6 13.0 %copy-start.20 = (bf16[128,768]{1,0:T(8,128)(2,1)}, bf16[128,768]{1,0:T(8,128)(2,1)S(1)}, u32[]{:S(2)}) copy-start(bf16[128,768]{1,0:T(8,128)(2,1)S(1)} %fusion.22) | copy-start | bytes 589828
  53.4 22.3 %copy-start.12 = (bf16[128,768]{0,1:T(8,128)(2,1)}, bf16[128,768]{0,1:T(8,128)(2,1)S(1)}, u32[]{:S(2)}) copy-start(bf16[128,768]{0,1:T(8,128)(2,1)S(1)} %copy.67) | copy-start | bytes 589828
  64.6 16.6 %copy-start.19 = (bf16[512,768]{0,1:T(8,128)(2,1)}, bf16[512,768]{0,1:T(8,128)(2,1)S(1)}, u32[]{:S(2)}) copy-start(bf16[512,768]{0,1:T(8,128)(2,1)S(1)} %copy.66) | copy-start | bytes 2359300
  88.8 45.1 %copy-start.55 = (f32[128]{0:T(128)}, f32[128]{0:T(128)S(1)}, u32[]{:S(2)}) copy-start(f32[128]{0:T(128)S(1)} %get-tuple-element.63) | copy-start | bytes 1540
  88.8 45.1 %copy-start.38 = (f32[128]{0:T(128)}, f32[128]{0:T(128)S(1)}, u32[]{:S(2)}) copy-start(f32[128]{0:T(128)S(1)} %fusion.107) | copy-start | bytes 1540
  90.7 109.2 %copy-start.24 = (f32[128]{0:T(128)}, f32[128]{0:T(128)S(1)}, u32[]{:S(2)}) copy-start(f32[128]{0:T(128)S(1)} %get-tuple-element.65) | copy-start | bytes 1540
  90.8 109.2 %copy-start.32 = (f32[128]{0:T(128)}, f32[128]{0:T(128)S(1)}, u32[]{:S(2)}) copy-start(f32[128]{0:T(128)S(1)} %fusion.111) | copy-start | bytes 1540
  224.0 114.0 %copy-start.2 = (f32[128,768]{1,0:T(8,128)}, f32[128,768]{1,0:T(8,128)S(1)}, u32[]{:S(2)}) copy-start(f32[128,768]{1,0:T(8,128)S(1)} %get-tuple-element.59) | copy-start | bytes 1179652
  233.8 49.3 %reduce-scatter.31.cloned.1.call-start = ((), (), s32[]{:S(2)}) async-start(), calls=%async_computation.20 | async-start | bytes 983040
  243.6 104.8 %reduce-scatter.19.cloned.1.call-start = ((), (), s32[]{:S(2)}) async-start(), calls=%async_computation.14 | async-start | bytes 4423680 | tf_op jit(solution)/shard_map/reduce_scatter | solution.py:302
  287.1 121.8 %reduce-scatter.29.cloned.1.call-start = ((), (), s32[]{:S(2)}) async-start(), calls=%async_computation.19 | async-start | bytes 11796480 | tf_op jit(solution)/shard_map/reduce_scatter | solution.py:334
  290.4 34.0 %copy-start.17 = (bf16[2,68,768]{2,1,0:T(8,128)(2,1)S(1)}, bf16[2,68,768]{2,1,0:T(8,128)(2,1)}, u32[]{:S(2)}) copy-start(bf16[2,68,768]{2,1,0:T(8,128)(2,1)} %gather.24) | copy-start | bytes 626692
  290.4 34.0 %copy-start.49 = (bf16[2,68]{1,0:T(2,128)(2,1)S(1)}, bf16[2,68]{1,0:T(2,128)(2,1)}, u32[]{:S(2)}) copy-start(bf16[2,68]{1,0:T(2,128)(2,1)} %mul.339) | copy-start | bytes 820
  329.7 160.5 %reduce-scatter.27.cloned.1.call-start = ((), (), s32[]{:S(2)}) async-start(), calls=%async_computation.18 | async-start | bytes 11796480 | tf_op jit(solution)/shard_map/reduce_scatter | solution.py:320
  336.1 182.5 %reduce-scatter.23.cloned.1.call-start = ((), (), s32[]{:S(2)}) async-start(), calls=%async_computation.16 | async-start | bytes 1474560 | tf_op jit(solution)/shard_map/reduce_scatter | solution.py:314
  339.6 203.8 %reduce-scatter.37.cloned.1.call-start = ((), (), s32[]{:S(2)}) async-start(), calls=%async_computation.23 | async-start | bytes 491520
  340.9 225.4 %reduce-scatter.35.cloned.1.call-start = ((), (), s32[]{:S(2)}) async-start(), calls=%async_computation.22 | async-start | bytes 491520
  348.3 286.8 %reduce-scatter.21.cloned.1.call-start = ((), (), s32[]{:S(2)}) async-start(), calls=%async_computation.15 | async-start | bytes 1990656 | tf_op jit(solution)/shard_map/reduce_scatter | solution.py:351
  351.0 587.1 %all-reduce.9.cloned.1.call-start = ((), (), s32[]{:S(2)}) async-start(), calls=%async_computation.24 | async-start | bytes 18874368
  497.4 505.7 %reduce-scatter.25.cloned.1.call-start = ((), (), s32[]{:S(2)}) async-start(), calls=%async_computation.17 | async-start | bytes 663552 | tf_op jit(solution)/shard_map/reduce_scatter | solution.py:352
  529.9 14.4 %copy-start.54 = (f32[128]{0:T(128)S(1)}, f32[128]{0:T(128)}, u32[]{:S(2)}) copy-start(f32[128]{0:T(128)} %copy-done.53) | copy-start | bytes 1540
  530.0 14.5 %copy-start.3 = (f32[128,768]{1,0:T(8,128)S(1)}, f32[128,768]{1,0:T(8,128)}, u32[]{:S(2)}) copy-start(f32[128,768]{1,0:T(8,128)} %copy-done.2) | copy-start | bytes 1179652
  (46 other events, 165.3 us)
Sparse Core Ops, SparseCore 0:
  9.6 32.0 all-gather.6
  43.2 17.9 all-gather.8
  62.8 64.0 all-gather.10
  128.3 64.9 all-gather.12
  233.9 23.2 reduce-scatter.32
  259.8 23.2 reduce-scatter.30
  287.3 40.4 reduce-scatter.18
  330.5 78.4 reduce-scatter.28
  411.8 78.4 reduce-scatter.26
  492.8 25.6 reduce-scatter.22
  521.6 20.8 reduce-scatter.36
  545.5 20.8 reduce-scatter.34
  569.8 65.2 reduce-scatter.20
  639.5 298.5 all-reduce.8
  942.1 60.9 reduce-scatter.24
where the time goes:
time: 1020 us; the launch traced here: 1010 us
  waiting for transfers between devices  707 us (69%)
  local copies, waits for them, and re-layouts  112 us (11%)
  matrix products  80 us (8%)
  blocking collectives  62.6 us (6%)
  other arithmetic  31.1 us (3%)
  between operations  16.5 us (2%)
    unnamed x20, waiting for transfers between devices  359 us
    reduce_scatter x1, waiting for transfers between devices, local(): lax.psum_scatter(jnp.einsum('ecd,ecf->fed', tiles, grad_in, preferred_ele...  74.1 us
    reduce_scatter x1, waiting for transfers between devices, local(): lax.psum_scatter(out_share, 'rep', scatter_dimension=0, tiled=True)  61 us
    all_gather x1, waiting for transfers between devices, local(): lax.all_gather(w_out, 'fsdp', axis=1, tiled=True)  59.4 us
    reduce_scatter x1, waiting for transfers between devices, local(): lax.psum_scatter(jnp.einsum('ecf,ecd->fed', jnp.take(activation, picked,...  57.9 us
    reduce_scatter x1, waiting for transfers between devices, local(): lax.psum_scatter(qkv_share, 'rep', scatter_dimension=0, tiled=True)  49.2 us
    all_gather x1, waiting for transfers between devices, local(): lax.all_gather(w_in, 'fsdp', axis=2, tiled=True)  36.1 us
    gather x1, local copies, waits for them, and re-layouts, local(): jnp.take(activation, picked, axis=2)  21.9 us
  transfers between devices with their start and end apart: 15, of which 11 were waited for; matrix products, arithmetic and copies ran while one was open for 17% of the time, Pallas kernels for 0%

commit v1 on v0

v1 whole, which is shorter than its diff:
```python
from functools import partial

import jax
import jax.numpy as jnp
from jax import lax
from jax.experimental import pallas as pl
from jax.experimental.pallas import tpu as pltpu
from jax.sharding import PartitionSpec as P

D = 768
H = 12
HD = 64
FF = 3072
NB = 32
EXPERTS = 2

NORM_EPSILON = 1e-06
SCORE_SCALE = 0.125
MASKED_SCORE = -1000000000.0
HIGHEST_PRECISION = lax.Precision.HIGHEST
BF = jnp.bfloat16
F32 = jnp.float32


def norm_rows(values, weights):
    return (
        values
        * lax.rsqrt(jnp.mean(values * values, axis=-1, keepdims=True) + NORM_EPSILON)
        * weights
    )


def product(left, right):
    return jnp.dot(left, right, preferred_element_type=F32)


def product_tn(left, right):
    return lax.dot_general(left, right, (((0,), (0,)), ((), ())), preferred_element_type=F32)


def product_nt(left, right):
    return lax.dot_general(left, right, (((1,), (1,)), ((), ())), preferred_element_type=F32)


def forward_kernel(
    lengths, x_ref, gain_ref, w_ref, along_ref, xn_ref, q_ref, k_ref, v_ref, p_ref, a_ref
):
    rows = x_ref.shape[0]
    span = along_ref.shape[1]
    normed = norm_rows(x_ref[...].astype(F32), gain_ref[...].astype(F32)).astype(BF)
    xn_ref[...] = normed
    q_ref[...] = product(normed, w_ref[0]).astype(BF)
    k_ref[...] = product(normed, w_ref[1]).astype(BF)
    v_ref[...] = product(normed, w_ref[2]).astype(BF)
    end_one = lengths[0, 0]
    end_two = end_one + lengths[0, 1]

    def segment(place):
        return (place >= end_one).astype(jnp.int32) + (place >= end_two).astype(jnp.int32)

    seg_rows = segment(lax.broadcasted_iota(jnp.int32, (rows, 1), 0))
    seg_cols = segment(lax.broadcasted_iota(jnp.int32, (1, rows), 1))
    same = seg_rows == seg_cols
    low_row = lax.broadcasted_iota(jnp.int32, (8, span), 0)
    for head in range(p_ref.shape[0]):
        cols = slice(head * HD, (head + 1) * HD)
        start = jnp.broadcast_to(along_ref[head : head + 1, :], (8, span))
        grown = pltpu.roll(start, span - (rows - 1), 1)
        for step in (1, 2, 4):
            grown = jnp.where((low_row & step) != 0, pltpu.roll(grown, step, 1), grown)
        step = 8
        while step < rows:
            grown = jnp.concatenate([grown, pltpu.roll(grown, step, 1)], axis=0)
            step *= 2
        scores = (
            product_nt(q_ref[:, cols], k_ref[:, cols]) * SCORE_SCALE + grown[:, :rows]
        )
        scores = jnp.where(same, scores, MASKED_SCORE)
        raised = jnp.exp(scores - jnp.max(scores, axis=-1, keepdims=True))
        probs = raised / jnp.sum(raised, axis=-1, keepdims=True)
        p_ref[head] = probs
        a_ref[:, cols] = product(probs.astype(BF), v_ref[:, cols]).astype(BF)


def backward_kernel(q_ref, k_ref, v_ref, p_ref, da_ref, dq_ref, dk_ref, dv_ref, along_ref):
    rows = q_ref.shape[0]
    span = along_ref.shape[1]
    low_row = lax.broadcasted_iota(jnp.int32, (8, span), 0)
    along_ref[...] = jnp.zeros_like(along_ref)
    for head in range(p_ref.shape[0]):
        cols = slice(head * HD, (head + 1) * HD)
        probs = p_ref[head]
        grad_att = da_ref[:, cols]
        grad_probs = product_nt(grad_att, v_ref[:, cols])
        total = jnp.sum(probs * grad_probs, axis=-1, keepdims=True)
        grad_scores = (probs * (grad_probs - total)).astype(BF)
        dq_ref[:, cols] = (product(grad_scores, k_ref[:, cols]) * SCORE_SCALE).astype(BF)
        dk_ref[:, cols] = (product_tn(grad_scores, q_ref[:, cols]) * SCORE_SCALE).astype(BF)
        dv_ref[:, cols] = product_tn(probs.astype(BF), grad_att).astype(BF)
        folded = jnp.concatenate(
            [grad_scores.astype(F32), jnp.zeros((rows, span - rows), F32)], axis=1
        )
        half = rows // 2
        while half >= 8:
            folded = folded[:half] + pltpu.roll(folded[half:], span - half, 1)
            half //= 2
        for step in (1, 2, 4):
            folded = jnp.where((low_row & step) != 0, pltpu.roll(folded, span - step, 1), folded)
        summed = pltpu.roll(folded, rows - 1, 1)
        along_ref[head : head + 1, :] = jnp.sum(summed, axis=0, keepdims=True)


def rep_reduce(blocks, order):
    count = blocks.shape[0]
    bits = count.bit_length() - 1
    me = lax.axis_index("rep")
    rest = blocks.shape[1:]
    value = blocks.reshape((2,) * bits + rest)
    left = list(range(bits - 1, -1, -1))
    for bit in order:
        axis = left.index(bit)
        mine = (me >> bit) & 1
        send = lax.dynamic_index_in_dim(value, 1 - mine, axis, keepdims=False).astype(BF)
        keep = lax.dynamic_index_in_dim(value, mine, axis, keepdims=False).astype(F32)
        taken = lax.ppermute(send, "rep", [(i, i ^ (1 << bit)) for i in range(count)])
        value = keep + taken.astype(F32)
        left.remove(bit)
    return value


def to_owner(value):
    rep_count = lax.axis_size("rep")
    fsdp_count = lax.axis_size("fsdp")
    pairs = [
        (r * fsdp_count + f, f * rep_count + r)
        for r in range(rep_count)
        for f in range(fsdp_count)
    ]
    return lax.ppermute(value.astype(BF), ("rep", "fsdp"), pairs).astype(F32)


def local(
    tokens,
    expert_ids,
    seq_lengths,
    rel_buckets,
    attn_qkv,
    attn_out,
    norm_gains,
    bias_table,
    router,
    w_in,
    w_out,
    cotangent,
):
    rows = tokens.shape[0]
    fc = lax.axis_size("fsdp")
    rc = lax.axis_size("rep")
    f = lax.axis_index("fsdp")
    group = rows * fc
    width = D // fc
    heads = H // fc
    span = 2 * group

    vm = pl.BlockSpec(memory_space=pltpu.VMEM)
    bits = rc.bit_length() - 1
    x_first = list(range(bits))
    z_first = ([1, 0] + list(range(2, bits))) if bits > 1 else x_first

    def own(values):
        return lax.dynamic_slice_in_dim(values, f * rows, rows, 0)

    n_gain, n_table, n_router = 2 * width, NB // fc * H, width * EXPERTS
    small = jnp.concatenate(
        [
            norm_gains.reshape(-1),
            bias_table.reshape(-1),
            router.reshape(-1),
            expert_ids[:, 0].astype(BF),
        ]
    )
    small = jnp.pad(small, (0, 2 * D - small.shape[0]))[None]
    pack = jnp.concatenate(
        [
            jnp.concatenate([tokens, cotangent], axis=1),
            jnp.pad(small, ((0, 15), (0, 0))),
        ],
        axis=0,
    )
    got = lax.all_gather(pack, "fsdp")
    x_all = got[:, :rows, :D].reshape(group, D)
    g_all = got[:, :rows, D:].reshape(group, D).astype(F32)
    sm = got[:, rows]
    gains = sm[:, :n_gain].reshape(fc, 2, width).transpose(1, 0, 2).reshape(2, D)
    at = n_gain
    table = sm[:, at : at + n_table].reshape(NB, H)
    at += n_table
    router_full = sm[:, at : at + n_router].reshape(D, EXPERTS)
    at += n_router
    ids_all = sm[:, at : at + rows].reshape(group, 1).astype(F32)

    cut = attn_qkv.reshape(3, width, fc, width).transpose(2, 0, 1, 3)
    qkv_cols = lax.all_to_all(cut, "fsdp", 0, 0, tiled=True)
    qkv_cols = qkv_cols.transpose(1, 0, 2, 3).reshape(3, D, width)
    out_full = lax.all_gather(attn_out, "fsdp", axis=0, tiled=True)

    codes = (
        jnp.pad(rel_buckets, (0, 1))[:, None] == jnp.arange(NB, dtype=jnp.int32)[None, :]
    )
    table_own = lax.dynamic_slice_in_dim(table, f * heads, heads, 1)
    along = lax.dot_general(
        table_own, codes.astype(BF), (((0,), (1,)), ((), ())), preferred_element_type=F32
    )
    along = jnp.pad(along, ((0, 8 - heads), (0, 0)))

    head_type = jax.ShapeDtypeStruct((group, width), BF)
    normed, queries, keys, values, probs, attended = pl.pallas_call(
        forward_kernel,
        in_specs=[pl.BlockSpec(memory_space=pltpu.SMEM), vm, vm, vm, vm],
        out_specs=[vm] * 6,
        out_shape=[
            jax.ShapeDtypeStruct((group, D), BF),
            head_type,
            head_type,
            head_type,
            jax.ShapeDtypeStruct((heads, group, group), F32),
            head_type,
        ],
        compiler_params=pltpu.CompilerParams(vmem_limit_bytes=40 << 20),
        name="attention_forward",
    )(seq_lengths, x_all, gains[:1], qkv_cols, along)

    attended_all = lax.all_gather(attended, "fsdp").transpose(1, 0, 2).reshape(group, D)
    inputs = x_all.astype(F32)
    hidden = inputs + product(attended_all, out_full)
    gain_two = gains[1].astype(F32)
    hn = norm_rows(hidden, gain_two).astype(BF)
    logits = product(hn, router_full)

    def gate_of(values, marks):
        return jnp.sum(jax.nn.softmax(values, axis=-1) * marks, axis=1, keepdims=True)

    chosen = (ids_all == jnp.arange(EXPERTS, dtype=F32)[None, :]).astype(F32)
    gating = gate_of(logits, chosen)
    grad_routed = (gating * g_all).astype(BF)
    first = ids_all == 0.0
    gelu = partial(jax.nn.gelu, approximate=True)
    u = jnp.where(first, product(hn, w_in[0]), product(hn, w_in[1]))
    act, gelu_pull = jax.vjp(gelu, u)
    act = act.astype(BF)
    none = jnp.zeros((), BF)
    act_zero = jnp.where(first, act, none)
    act_one = jnp.where(first, none, act)
    routed_part = product(act_zero, w_out[0]) + product(act_one, w_out[1])
    grad_act = jnp.where(
        first, product_nt(grad_routed, w_out[0]), product_nt(grad_routed, w_out[1])
    )
    grad_u = gelu_pull(grad_act)[0].astype(BF)
    u_zero = jnp.where(first, grad_u, none)
    u_one = jnp.where(first, none, grad_u)
    hn_part = product_nt(u_zero, w_in[0]) + product_nt(u_one, w_in[1])
    parts = jnp.concatenate([routed_part.astype(BF), hn_part.astype(BF)], axis=1)
    parts = lax.all_to_all(parts.reshape(fc, rows, 2 * D), "fsdp", 0, 0, tiled=True)
    sums = jnp.sum(parts.astype(F32), axis=0)
    routed, grad_hn = sums[:, :D], sums[:, D:]

    def blocks_of(pieces, count):
        return jnp.stack(
            [piece.astype(BF).reshape(rc, piece.shape[0] // rc, piece.shape[1]) for piece in pieces],
            axis=1,
        )

    in_share = rep_reduce(
        blocks_of([product_tn(hn, u_zero), product_tn(hn, u_one)], rc), x_first
    )
    outer_share = rep_reduce(
        blocks_of([product_tn(act_zero, grad_routed), product_tn(act_one, grad_routed)], rc),
        z_first,
    )
    grad_w_out = to_owner(outer_share)

    hidden_own = own(hidden)
    hn_own = own(hn)
    logits_own = own(logits)
    chosen_own = own(chosen)
    gating_own = own(gating)
    grad_mixed = cotangent.astype(F32)
    mixed = (hidden_own + gating_own * routed).astype(BF)
    grad_gate = jnp.sum(grad_mixed * routed, axis=1, keepdims=True)
    grad_logits = jax.vjp(lambda z: gate_of(z, chosen_own), logits_own)[1](grad_gate)[0]
    router_wide = router_full.astype(F32)
    grad_hn = grad_hn + (
        grad_logits[:, :1] * router_wide[:, 0][None] + grad_logits[:, 1:] * router_wide[:, 1][None]
    )
    grad_router = lax.dot_general(
        hn_own.astype(F32),
        grad_logits,
        (((0,), (0,)), ((), ())),
        precision=HIGHEST_PRECISION,
        preferred_element_type=F32,
    )
    grad_hidden_part, grad_gain_two = jax.vjp(norm_rows, hidden_own, gain_two)[1](grad_hn)
    grad_hidden = grad_mixed + grad_hidden_part
    branch_all = lax.all_gather(grad_hidden.astype(BF), "fsdp", axis=0, tiled=True)
    grad_attended = product_nt(branch_all, attn_out).astype(BF)
    out_part = product_tn(attended, branch_all).astype(BF)
    out_share = to_owner(rep_reduce(out_part.reshape(rc, width // rc, D), x_first))

    grad_q, grad_k, grad_v, grad_along = pl.pallas_call(
        backward_kernel,
        in_specs=[vm] * 5,
        out_specs=[vm] * 4,
        out_shape=[
            head_type,
            head_type,
            head_type,
            jax.ShapeDtypeStruct((8, span), F32),
        ],
        compiler_params=pltpu.CompilerParams(vmem_limit_bytes=40 << 20),
        name="attention_backward",
    )(queries, keys, values, probs, grad_attended)

    xn_part = (
        product_nt(grad_q, qkv_cols[0])
        + product_nt(grad_k, qkv_cols[1])
        + product_nt(grad_v, qkv_cols[2])
    ).astype(BF)
    xn_parts = lax.all_to_all(xn_part.reshape(fc, rows, D), "fsdp", 0, 0, tiled=True)
    grad_normed = jnp.sum(xn_parts.astype(F32), axis=0)

    grad_stack = jnp.concatenate([grad_q, grad_k, grad_v], axis=1)
    qkv_part = product_tn(normed, grad_stack).astype(BF)
    qkv_share = rep_reduce(qkv_part.reshape(rc, D // rc, 3 * width), x_first)
    piece = D // (rc * fc)
    qkv_share = lax.all_to_all(
        qkv_share.astype(BF).reshape(fc, piece, 3 * width), "fsdp", 0, 0, tiled=True
    )
    grad_qkv = (
        qkv_share.astype(F32)
        .reshape(fc, piece, 3, width)
        .transpose(2, 1, 0, 3)
        .reshape(3, piece, D)
    )

    gain_one = gains[0].astype(F32)
    grad_input_part, grad_gain_one = jax.vjp(norm_rows, tokens.astype(F32), gain_one)[1](
        grad_normed
    )
    grad_tokens = grad_hidden + grad_input_part
    table_own_grad = lax.dot_general(
        codes.astype(F32),
        grad_along[:heads],
        (((0,), (1,)), ((), ())),
        precision=HIGHEST_PRECISION,
        preferred_element_type=F32,
    )
    table_grad = lax.dynamic_update_slice_in_dim(
        jnp.zeros((NB, H), F32), table_own_grad, f * heads, 1
    )
    little = jnp.concatenate(
        [
            grad_gain_one,
            grad_gain_two,
            grad_router.T.reshape(-1),
            table_grad.reshape(-1),
        ]
    ).reshape(-1, 128)
    little = lax.psum(little, ("rep", "fsdp")).reshape(-1)
    grad_gains = lax.dynamic_slice_in_dim(little[: 2 * D].reshape(2, D), f * width, width, 1)
    grad_router = lax.dynamic_slice_in_dim(
        little[2 * D : 4 * D].reshape(EXPERTS, D), f * width, width, 1
    ).T
    grad_table = lax.dynamic_slice_in_dim(
        little[4 * D :].reshape(NB, H), f * (NB // fc), NB // fc, 0
    )
    return (
        mixed,
        grad_tokens,
        grad_qkv,
        out_share,
        grad_gains,
        grad_table,
        grad_router,
        in_share,
        grad_w_out,
    )


def solution(mesh):
    return jax.shard_map(
        local,
        mesh=mesh,
        in_specs=(
            P(("rep", "fsdp"), None),
            P(("rep", "fsdp"), None),
            P("rep", None),
            P(),
            P(None, "fsdp", None),
            P("fsdp", None),
            P(None, "fsdp"),
            P("fsdp", None),
            P("fsdp", None),
            P(None, None, "fsdp"),
            P(None, "fsdp", None),
            P(("rep", "fsdp"), None),
        ),
        out_specs=(
            P(("rep", "fsdp"), None),
            P(("rep", "fsdp"), None),
            P(None, ("rep", "fsdp"), None),
            P(("rep", "fsdp"), None),
            P(None, "fsdp"),
            P("fsdp", None),
            P("fsdp", None),
            P(None, "rep", "fsdp"),
            P(None, ("rep", "fsdp"), None),
        ),
        check_vma=False,
    )
```

time: 1020 us -> 308 us (0.30)
  waiting for transfers between devices: 707 us -> 82.1 us
  local copies, waits for them, and re-layouts: 112 us -> 41.5 us
  matrix products: 80 us -> 26.7 us
  starting transfers between devices: 0.78 us -> 33 us
    unnamed x20 -> x2, waiting for transfers between devices: 359 us -> 0.71 us
    reduce_scatter x6 -> x0, waiting for transfers between devices: 252 us -> none  [the longest x1 74.1 us: local(): lax.psum_scatter(jnp.einsum('ecd,ecf->fed', tiles, grad_in, preferred_ele...]
    all_gather x4 -> x2, waiting for transfers between devices: 95.5 us -> 0.02 us  [the longest x1 0.02 us: local(): got = lax.all_gather(pack, 'fsdp')]
    dot_general x20 -> x9, matrix products: 67.4 us -> 9.57 us  [the longest x6 6.3 us: product(): return jnp.dot(left, right, preferred_element_type=F32)]
    ppermute x0 -> x14, waiting for transfers between devices: none -> 49.2 us  [the longest x12 32.9 us: rep_reduce(): taken = lax.ppermute(send, 'rep', [(i, i ^ 1 << bit) for i in range(count)])]
    gather x8 -> x0, local copies, waits for them, and re-layouts: 33 us -> none  [the longest x1 21.9 us: local(): jnp.take(activation, picked, axis=2)]
    all_to_all x0 -> x4, waiting for transfers between devices: none -> 32.1 us  [the longest x1 23.8 us: local(): qkv_cols = lax.all_to_all(cut, 'fsdp', 0, 0, tiled=True)]
    psum x1, blocking collectives: 18.6 us -> 43.9 us  [local(): little = lax.psum(little, ('rep', 'fsdp')).reshape(-1)]
  transfers between devices with their start and end apart: 15 -> 20, of which waited for: 11 -> 7; matrix products, arithmetic and copies ran while one was open for 17% -> 20% of each run, Pallas kernels for 0% -> 3%
where the time goes in v1:
time: 308 us; the launch traced here: 307 us
  waiting for transfers between devices  82.1 us (27%)
  blocking collectives  64.3 us (21%)
  local copies, waits for them, and re-layouts  41.5 us (13%)
  other arithmetic  35.8 us (12%)
  starting transfers between devices  33 us (11%)
  matrix products  26.7 us (9%)
  between operations  15.1 us (5%)
  Pallas kernels  8.06 us (3%)
    psum x1, blocking collectives, local(): little = lax.psum(little, ('rep', 'fsdp')).reshape(-1)  43.9 us
    ppermute x12, waiting for transfers between devices, rep_reduce(): taken = lax.ppermute(send, 'rep', [(i, i ^ 1 << bit) for i in range(count)])  32.9 us
    all_to_all x1, waiting for transfers between devices, local(): qkv_cols = lax.all_to_all(cut, 'fsdp', 0, 0, tiled=True)  23.8 us
    unnamed x142, local copies, waits for them, and re-layouts  17.4 us
    ppermute x2, waiting for transfers between devices, to_owner(): return lax.ppermute(value.astype(BF), ('rep', 'fsdp'), pairs).astype(F32)  16.3 us
    ppermute x12, starting transfers between devices, rep_reduce(): taken = lax.ppermute(send, 'rep', [(i, i ^ 1 << bit) for i in range(count)])  12.8 us
    all_gather x1, blocking collectives, local(): lax.all_gather(attended, 'fsdp').transpose(1, 0, 2).reshape(group, D)  12.3 us
    add x9, other arithmetic, rep_reduce(): value = keep + taken.astype(F32)  9.89 us
  transfers between devices with their start and end apart: 20, of which 7 were waited for; matrix products, arithmetic and copies ran while one was open for 20% of the time, Pallas kernels for 3%

profile of v1, /device:TPU:2, one launch (start us, length us, event | category | flops | bytes accessed | tf_op | source)
XLA Modules:
  0.0 306.6 jit_solution(17958978422608818472)
XLA Ops:
  10.6 1.8 fusion.43
  14.7 3.7 %all-to-all-start = ((bf16[4,3,192,192]{3,2,1,0:T(8,128)(2,1)}), bf16[4,3,192,192]{3,2,1,0:T(8,128)(2,1)S(1)}, u32[]{:S(2)}, u32[]{:S(2)}) async-start(bf16[4,3,192,192]{3,2,1,0:T(8,128)(2,1)} %copy.87), calls=%async_computation | async-start | bytes 2359296 | tf_op jit(solution)/shard_map/all_to_all | solution.py:203
  19.9 23.8 %all-to-all-done = bf16[4,3,192,192]{3,2,1,0:T(8,128)(2,1)S(1)} async-done(((bf16[4,3,192,192]{3,2,1,0:T(8,128)(2,1)}), bf16[4,3,192,192]{3,2,1,0:T(8,128)(2,1)S(1)}, u32[]{:S(2)}, u32[]{:S(2)}) %all-to-all-start) | async-done | bytes 884768 | tf_op jit(solution)/shard_map/all_to_all | solution.py:203
  48.6 4.2 %attention_forward.1 = (bf16[512,768]{1,0:T(8,128)(2,1)S(1)}, bf16[512,192]{1,0:T(8,128)(2,1)S(1)}, bf16[512,192]{1,0:T(8,128)(2,1)S(1)}, bf16[512,192]{1,0:T(8,...) custom-call(s32[1,2]{1,0:T(1,128)S(1)} %copy-done.16, bf16[512,768]{1,0:T(8,128)(2,1)S(1)} %bitcast.163, ...), custom_call_target="tpu_custom_call" | custom-call | tf_op jit(solution)/shard_map/attention_forward/pallas_call | solution.py:217
  52.8 1.7 copy-done
  56.0 12.3 %all-gather.1 = bf16[2048,192]{1,0:T(8,128)(2,1)S(1)} all-gather(bf16[512,192]{1,0:T(8,128)(2,1)S(1)} %get-tuple-element.19), channel_id=3, replica_groups=mesh['rep'=8,'fsdp'=4] {'fsdp'}, dimensions={0}, use_global_device_ids=true | all-gather | bytes 983040 | tf_op jit(solution)/shard_map/all_gather | solution.py:233
  72.2 2.4 multiply_reduce_fusion
  84.3 1.9 convolution_convert_fusion.3
  86.2 1.9 convolution_convert_fusion.2
  89.1 2.0 convolution_convert_fusion.1
  91.1 1.9 convolution_convert_fusion
  96.0 3.8 %all-to-all-start.1 = ((bf16[4,128,1536]{2,1,0:T(8,128)(2,1)}), bf16[4,128,1536]{2,1,0:T(8,128)(2,1)S(1)}, u32[]{:S(2)}, u32[]{:S(2)}) async-start(bf16[4,128,1536]{2,1,0:T(8,128)(2,1)} %bitcast.19), calls=%async_computation.1 | async-start | bytes 3145728 | tf_op jit(solution)/shard_map/all_to_all | solution.py:263
  99.8 2.9 fusion.11
  111.3 8.3 %all-to-all-done.1 = bf16[4,128,1536]{2,1,0:T(8,128)(2,1)S(1)} async-done(((bf16[4,128,1536]{2,1,0:T(8,128)(2,1)}), bf16[4,128,1536]{2,1,0:T(8,128)(2,1)S(1)}, u32[]{:S(2)}, u32[]{:S(2)}) %all-to-all-start.1) | async-done | bytes 1572896 | tf_op jit(solution)/shard_map/all_to_all | solution.py:263
  120.9 2.2 fusion.93
  123.2 8.1 %all_gather.23 = bf16[512,768]{1,0:T(8,128)(2,1)S(1)} all-gather(bf16[128,768]{1,0:T(8,128)(2,1)S(1)} %get-tuple-element.37), channel_id=1, replica_groups=mesh['rep'=8,'fsdp'=4] {'fsdp'}, dimensions={0}, use_global_device_ids=true | all-gather | bytes 983040 | tf_op jit(solution)/shard_map/all_gather | solution.py:304
  137.2 3.9 %attention_backward.1 = (bf16[512,192]{1,0:T(8,128)(2,1)S(1)}, bf16[512,192]{1,0:T(8,128)(2,1)S(1)}, bf16[512,192]{1,0:T(8,128)(2,1)S(1)}, f32[8,1024]{1,0:T(8,128)S(1)}) custom-call(bf16[512,192]{1,0:T(8,128)(2,1)S(1)} %copy-done.5, bf16[512,192]{1,0:T(8,128)(2,1)S(1)} %copy-done.7, bf16[512,192]{1,0:T(8,128)(2,1)S(1)} %copy-done.9, ...), custom_call_target="tpu_custom_call" | custom-call | tf_op jit(solution)/shard_map/attention_backward/pallas_call | solution.py:309
  144.1 4.3 %all-to-all-start.2 = ((bf16[4,128,768]{2,1,0:T(8,128)(2,1)}), bf16[4,128,768]{2,1,0:T(8,128)(2,1)}, u32[]{:S(2)}, u32[]{:S(2)}) async-start(bf16[4,128,768]{2,1,0:T(8,128)(2,1)} %bitcast.25), calls=%async_computation.2 | async-start | bytes 1572864 | tf_op jit(solution)/shard_map/all_to_all | solution.py:328
  148.5 1.8 convolution_convert_fusion.4
  160.7 9.0 %collective-permute-done.3 = bf16[2,2,24,768]{3,2,0,1:T(8,128)(2,1)S(1)} collective-permute-done((bf16[2,2,24,768]{3,2,0,1:T(8,128)(2,1)S(1)}, bf16[2,2,24,768]{3,2,0,1:T(8,128)(2,1)S(1)}, u32[]{:S(2)}, u32[]{:S(2)}) %collective-permute-start.3) | collective-permute-done | bytes 147488 | tf_op jit(solution)/shard_map/ppermute | solution.py:125
  172.5 2.1 collective-permute-done.4
  174.6 2.5 collective-permute-start.5
  177.1 1.7 fusion.58
  181.3 1.9 collective-permute-start.6
  184.1 4.9 %collective-permute-done.6 = bf16[24,768]{1,0:T(8,128)(2,1)S(1)} collective-permute-done((bf16[24,768]{1,0:T(8,128)(2,1)S(1)}, bf16[24,768]{1,0:T(8,128)(2,1)S(1)}, u32[]{:S(2)}, u32[]{:S(2)}) %collective-permute-start.6) | collective-permute-done | bytes 36896 | tf_op jit(solution)/shard_map/ppermute | solution.py:139
  195.9 43.9 %psum.7 = f32[27,128]{1,0:T(8,128)S(1)} all-reduce(f32[27,128]{1,0:T(8,128)S(1)} %maximum_bitcast_fusion), channel_id=1, replica_groups=mesh['rep'=8,'fsdp'=4] {'rep','fsdp'}, use_global_device_ids=true, to_apply=%region_16.17 | all-reduce | flops 3456 | bytes 27648 | tf_op jit(solution)/shard_map/psum | solution.py:368
  246.8 2.8 collective-permute-start.12
  253.0 21.8 %collective-permute-done.2 = bf16[96,576]{1,0:T(8,128)(2,1)S(1)} collective-permute-done((bf16[96,576]{1,0:T(8,128)(2,1)S(1)}, bf16[96,576]{1,0:T(8,128)(2,1)S(1)}, u32[]{:S(2)}, u32[]{:S(2)}) %collective-permute-start.2) | collective-permute-done | bytes 110624 | tf_op jit(solution)/shard_map/ppermute | solution.py:125
  275.5 3.3 %all-to-all-start.3 = ((bf16[4,24,576]{2,1,0:T(8,128)(2,1)}), bf16[4,24,576]{2,1,0:T(8,128)(2,1)S(1)}, u32[]{:S(2)}, u32[]{:S(2)}) async-start(bf16[4,24,576]{2,1,0:T(8,128)(2,1)} %bitcast.33), calls=%async_computation.3 | async-start | bytes 245760 | tf_op jit(solution)/shard_map/all_to_all | solution.py:335
  279.9 3.2 %collective-permute-start.13 = (bf16[2,96,768]{2,1,0:T(8,128)(2,1)S(1)}, bf16[2,96,768]{2,1,0:T(8,128)(2,1)S(1)}, u32[]{:S(2)}, u32[]{:S(2)}) collective-permute-start(bf16[2,96,768]{2,1,0:T(8,128)(2,1)S(1)} %fusion.40), channel_id=1, source_target_pairs={{0,0},{1,8},{2,16},{3,24},{4,1},{5,9},{6,17},{7,25},{8,2},{9,10},{... | collective-permute-start | bytes 884744 | tf_op jit(solution)/shard_map/ppermute | solution.py:139
  285.7 1.8 bitcast_add_fusion.3
  287.6 11.3 %collective-permute-done.13 = bf16[2,96,768]{2,1,0:T(8,128)(2,1)S(1)} collective-permute-done((bf16[2,96,768]{2,1,0:T(8,128)(2,1)S(1)}, bf16[2,96,768]{2,1,0:T(8,128)(2,1)S(1)}, u32[]{:S(2)}, u32[]{:S(2)}) %collective-permute-start.13) | collective-permute-done | bytes 294944 | tf_op jit(solution)/shard_map/ppermute | solution.py:139
  (283 shorter events, 88.3 us)
Async XLA Ops:
  7.2 37.6 %all-gather.7.cloned.1.call-start = ((), (), s32[]{:S(2)}) async-start(), calls=%async_computation.5 | async-start | bytes 2211840 | tf_op jit(solution)/shard_map/all_gather | solution.py:190
  14.7 29.0 %all-to-all-start = ((bf16[4,3,192,192]{3,2,1,0:T(8,128)(2,1)}), bf16[4,3,192,192]{3,2,1,0:T(8,128)(2,1)S(1)}, u32[]{:S(2)}, u32[]{:S(2)}) async-start(bf16[4,3,192,192]{3,2,1,0:T(8,128)(2,1)} %copy.87), calls=%async_computation | async-start | bytes 2359296 | tf_op jit(solution)/shard_map/all_to_all | solution.py:203
  18.3 53.9 %all-gather.5.cloned.1.call-start = ((), (), s32[]{:S(2)}) async-start(), calls=%async_computation.4 | async-start | bytes 1474560 | tf_op jit(solution)/shard_map/all_gather | solution.py:205
  19.1 27.5 %copy-start.56 = (s32[1024]{0:T(1024)}, s32[1024]{0:T(1024)S(1)}, u32[]{:S(2)}) copy-start(s32[1024]{0:T(1024)S(1)} %pad.18) | copy-start | bytes 12292
  19.3 24.4 %copy-start.61 = (f32[128]{0:T(128)}, f32[128]{0:T(128)S(1)}, u32[]{:S(2)}) copy-start(f32[128]{0:T(128)S(1)} %fusion.46) | copy-start | bytes 1540
  55.3 13.0 %copy-start.4 = (bf16[512,192]{1,0:T(8,128)(2,1)}, bf16[512,192]{1,0:T(8,128)(2,1)S(1)}, u32[]{:S(2)}) copy-start(bf16[512,192]{1,0:T(8,128)(2,1)S(1)} %get-tuple-element.20.q_ref) | copy-start | bytes 589828
  55.3 13.0 %copy-start.6 = (bf16[512,192]{1,0:T(8,128)(2,1)}, bf16[512,192]{1,0:T(8,128)(2,1)S(1)}, u32[]{:S(2)}) copy-start(bf16[512,192]{1,0:T(8,128)(2,1)S(1)} %get-tuple-element.21.k_ref) | copy-start | bytes 589828
  55.3 13.0 %copy-start.8 = (bf16[512,192]{1,0:T(8,128)(2,1)}, bf16[512,192]{1,0:T(8,128)(2,1)S(1)}, u32[]{:S(2)}) copy-start(bf16[512,192]{1,0:T(8,128)(2,1)S(1)} %get-tuple-element.22.v_ref) | copy-start | bytes 589828
  74.9 11.3 %copy-start.26 = (bf16[512,768]{1,0:T(8,128)(2,1)}, bf16[512,768]{1,0:T(8,128)(2,1)S(1)}, u32[]{:S(2)}) copy-start(bf16[512,768]{1,0:T(8,128)(2,1)S(1)} %multiply_convert_fusion.2) | copy-start | bytes 2359300
  96.0 23.6 %all-to-all-start.1 = ((bf16[4,128,1536]{2,1,0:T(8,128)(2,1)}), bf16[4,128,1536]{2,1,0:T(8,128)(2,1)S(1)}, u32[]{:S(2)}, u32[]{:S(2)}) async-start(bf16[4,128,1536]{2,1,0:T(8,128)(2,1)} %bitcast.19), calls=%async_computation.1 | async-start | bytes 3145728 | tf_op jit(solution)/shard_map/all_to_all | solution.py:263
  105.6 49.7 %collective-permute-start.7 = (bf16[2,2,2,96,768]{4,3,2,0,1:T(8,128)(2,1)}, bf16[2,2,2,96,768]{4,3,2,0,1:T(8,128)(2,1)}, u32[]{:S(2)}, u32[]{:S(2)}) collective-permute-start(bf16[2,2,2,96,768]{4,3,2,0,1:T(8,128)(2,1)} %bitcast.159), channel_id=1, source_target_pairs={{0,4},{4,0},{8,12},{12,8},{16,20},{20,16},{24,28},{28,24},{1,5},{5... | collective-permute-start | bytes 3538952 | tf_op jit(solution)/shard_map/ppermute | solution.py:125
  109.1 50.1 %collective-permute-start.10 = (bf16[2,2,2,96,768]{4,3,2,0,1:T(8,128)(2,1)}, bf16[2,2,2,96,768]{4,3,2,0,1:T(8,128)(2,1)}, u32[]{:S(2)}, u32[]{:S(2)}) collective-permute-start(bf16[2,2,2,96,768]{4,3,2,0,1:T(8,128)(2,1)} %bitcast.158), channel_id=1, source_target_pairs={{0,8},{4,12},{8,0},{12,4},{16,24},{20,28},{24,16},{28,20},{1,9},{5... | collective-permute-start | bytes 3538952 | tf_op jit(solution)/shard_map/ppermute | solution.py:125
  111.3 9.7 %copy-start.63 = (f32[128]{0:T(128)S(1)}, f32[128]{0:T(128)}, u32[]{:S(2)}) copy-start(f32[128]{0:T(128)} %dynamic-slice.3) | copy-start | bytes 1540
  120.1 12.1 %copy-start.45 = (bf16[192,768]{1,0:T(8,128)(2,1)S(1)}, bf16[192,768]{1,0:T(8,128)(2,1)}, u32[]{:S(2)}) copy-start(bf16[192,768]{1,0:T(8,128)(2,1)} %param.17) | copy-start | bytes 884740
  120.9 13.4 %copy-start.1 = (f32[3,512,512]{2,1,0:T(8,128)S(1)}, f32[3,512,512]{2,1,0:T(8,128)}, u32[]{:S(2)}) copy-start(f32[3,512,512]{2,1,0:T(8,128)} %copy-done) | copy-start | bytes 9437188
  144.1 48.4 %all-to-all-start.2 = ((bf16[4,128,768]{2,1,0:T(8,128)(2,1)}), bf16[4,128,768]{2,1,0:T(8,128)(2,1)}, u32[]{:S(2)}, u32[]{:S(2)}) async-start(bf16[4,128,768]{2,1,0:T(8,128)(2,1)} %bitcast.25), calls=%async_computation.2 | async-start | bytes 1572864 | tf_op jit(solution)/shard_map/all_to_all | solution.py:328
  152.8 36.9 %collective-permute-start = (bf16[2,2,96,576]{3,2,1,0:T(8,128)(2,1)}, bf16[2,2,96,576]{3,2,1,0:T(8,128)(2,1)}, u32[]{:S(2)}, u32[]{:S(2)}) collective-permute-start(bf16[2,2,96,576]{3,2,1,0:T(8,128)(2,1)} %dynamic-slice_bitcast_fusion), channel_id=1, source_target_pairs={{0,4},{4,0},{8,12},{12,8},{16,20},{20,16},{24,28},{28,24},{1,5},{5... | collective-permute-start | bytes 1327112 | tf_op jit(solution)/shard_map/ppermute | solution.py:125
  153.7 16.0 %collective-permute-start.3 = (bf16[2,2,24,768]{3,2,0,1:T(8,128)(2,1)S(1)}, bf16[2,2,24,768]{3,2,0,1:T(8,128)(2,1)S(1)}, u32[]{:S(2)}, u32[]{:S(2)}) collective-permute-start(bf16[2,2,24,768]{3,2,0,1:T(8,128)(2,1)S(1)} %bitcast.186), channel_id=1, source_target_pairs={{0,4},{4,0},{8,12},{12,8},{16,20},{20,16},{24,28},{28,24},{1,5},{5... | collective-permute-start | bytes 442376 | tf_op jit(solution)/shard_map/ppermute | solution.py:125
  156.8 15.7 %copy-start.19 = (f32[2,2,2,96,768]{4,3,2,0,1:T(8,128)}, f32[2,2,2,96,768]{4,3,2,0,1:T(8,128)S(1)}, u32[]{:S(2)}) copy-start(f32[2,2,2,96,768]{4,3,2,0,1:T(8,128)S(1)} %convert_add_fusion.1) | copy-start | bytes 7077892
  157.7 83.5 %collective-permute-start.8 = (bf16[2,2,96,768]{3,2,1,0:T(8,128)(2,1)}, bf16[2,2,96,768]{3,2,1,0:T(8,128)(2,1)}, u32[]{:S(2)}, u32[]{:S(2)}) collective-permute-start(bf16[2,2,96,768]{3,2,1,0:T(8,128)(2,1)} %fusion.38), channel_id=1, source_target_pairs={{0,8},{4,12},{8,0},{12,4},{16,24},{20,28},{24,16},{28,20},{1,9},{5... | collective-permute-start | bytes 1769480 | tf_op jit(solution)/shard_map/ppermute | solution.py:125
  159.2 12.1 %copy-start.57 = (s32[1024]{0:T(1024)S(1)}, s32[1024]{0:T(1024)}, u32[]{:S(2)}) copy-start(s32[1024]{0:T(1024)} %copy-done.56) | copy-start | bytes 12292
  169.8 4.8 %collective-permute-start.4 = (bf16[2,24,768]{2,1,0:T(8,128)(2,1)S(1)}, bf16[2,24,768]{2,1,0:T(8,128)(2,1)S(1)}, u32[]{:S(2)}, u32[]{:S(2)}) collective-permute-start(bf16[2,24,768]{2,1,0:T(8,128)(2,1)S(1)} %fusion.61), channel_id=1, source_target_pairs={{0,8},{4,12},{8,0},{12,4},{16,24},{20,28},{24,16},{28,20},{1,9},{5... | collective-permute-start | bytes 221192 | tf_op jit(solution)/shard_map/ppermute | solution.py:125
  174.6 5.8 %collective-permute-start.5 = (bf16[24,768]{1,0:T(8,128)(2,1)S(1)}, bf16[24,768]{1,0:T(8,128)(2,1)}, u32[]{:S(2)}, u32[]{:S(2)}) collective-permute-start(bf16[24,768]{1,0:T(8,128)(2,1)S(1)} %fusion.63), channel_id=1, source_target_pairs={{0,16},{4,20},{8,24},{12,28},{16,0},{20,4},{24,8},{28,12},{1,17},{... | collective-permute-start | bytes 110600 | tf_op jit(solution)/shard_map/ppermute | solution.py:125
  181.3 7.8 %collective-permute-start.6 = (bf16[24,768]{1,0:T(8,128)(2,1)S(1)}, bf16[24,768]{1,0:T(8,128)(2,1)S(1)}, u32[]{:S(2)}, u32[]{:S(2)}) collective-permute-start(bf16[24,768]{1,0:T(8,128)(2,1)S(1)} %fusion.62), channel_id=1, source_target_pairs={{0,0},{1,8},{2,16},{3,24},{4,1},{5,9},{6,17},{7,25},{8,2},{9,10},{... | collective-permute-start | bytes 110600 | tf_op jit(solution)/shard_map/ppermute | solution.py:139
  184.1 59.7 %collective-permute-start.11 = (bf16[2,2,96,768]{3,2,1,0:T(8,128)(2,1)}, bf16[2,2,96,768]{3,2,1,0:T(8,128)(2,1)}, u32[]{:S(2)}, u32[]{:S(2)}) collective-permute-start(bf16[2,2,96,768]{3,2,1,0:T(8,128)(2,1)} %fusion.39), channel_id=1, source_target_pairs={{0,4},{4,0},{8,12},{12,8},{16,20},{20,16},{24,28},{28,24},{1,5},{5... | collective-permute-start | bytes 1769480 | tf_op jit(solution)/shard_map/ppermute | solution.py:125
  192.5 58.0 %collective-permute-start.1 = (bf16[2,96,576]{2,1,0:T(8,128)(2,1)}, bf16[2,96,576]{2,1,0:T(8,128)(2,1)}, u32[]{:S(2)}, u32[]{:S(2)}) collective-permute-start(bf16[2,96,576]{2,1,0:T(8,128)(2,1)} %fusion.56), channel_id=1, source_target_pairs={{0,8},{4,12},{8,0},{12,4},{16,24},{20,28},{24,16},{28,20},{1,9},{5... | collective-permute-start | bytes 663560 | tf_op jit(solution)/shard_map/ppermute | solution.py:125
  243.6 42.2 %collective-permute-start.9 = (bf16[2,96,768]{2,1,0:T(8,128)(2,1)}, bf16[2,96,768]{2,1,0:T(8,128)(2,1)}, u32[]{:S(2)}, u32[]{:S(2)}) collective-permute-start(bf16[2,96,768]{2,1,0:T(8,128)(2,1)} %fusion.50), channel_id=1, source_target_pairs={{0,16},{4,20},{8,24},{12,28},{16,0},{20,4},{24,8},{28,12},{1,17},{... | collective-permute-start | bytes 884744 | tf_op jit(solution)/shard_map/ppermute | solution.py:125
  246.8 32.1 %collective-permute-start.12 = (bf16[2,96,768]{2,1,0:T(8,128)(2,1)}, bf16[2,96,768]{2,1,0:T(8,128)(2,1)}, u32[]{:S(2)}, u32[]{:S(2)}) collective-permute-start(bf16[2,96,768]{2,1,0:T(8,128)(2,1)} %fusion.51), channel_id=1, source_target_pairs={{0,16},{4,20},{8,24},{12,28},{16,0},{20,4},{24,8},{28,12},{1,17},{... | collective-permute-start | bytes 884744 | tf_op jit(solution)/shard_map/ppermute | solution.py:125
  249.6 29.2 %copy-start.28 = (f32[2,2,96,768]{3,2,1,0:T(8,128)S(1)}, f32[2,2,96,768]{3,2,1,0:T(8,128)}, u32[]{:S(2)}) copy-start(f32[2,2,96,768]{3,2,1,0:T(8,128)} %copy-done.27) | copy-start | bytes 3538948
  251.6 23.3 %collective-permute-start.2 = (bf16[96,576]{1,0:T(8,128)(2,1)S(1)}, bf16[96,576]{1,0:T(8,128)(2,1)S(1)}, u32[]{:S(2)}, u32[]{:S(2)}) collective-permute-start(bf16[96,576]{1,0:T(8,128)(2,1)S(1)} %fusion.60), channel_id=1, source_target_pairs={{0,16},{4,20},{8,24},{12,28},{16,0},{20,4},{24,8},{28,12},{1,17},{... | collective-permute-start | bytes 331784 | tf_op jit(solution)/shard_map/ppermute | solution.py:125
  275.5 8.9 %all-to-all-start.3 = ((bf16[4,24,576]{2,1,0:T(8,128)(2,1)}), bf16[4,24,576]{2,1,0:T(8,128)(2,1)S(1)}, u32[]{:S(2)}, u32[]{:S(2)}) async-start(bf16[4,24,576]{2,1,0:T(8,128)(2,1)} %bitcast.33), calls=%async_computation.3 | async-start | bytes 245760 | tf_op jit(solution)/shard_map/all_to_all | solution.py:335
  279.9 19.0 %collective-permute-start.13 = (bf16[2,96,768]{2,1,0:T(8,128)(2,1)S(1)}, bf16[2,96,768]{2,1,0:T(8,128)(2,1)S(1)}, u32[]{:S(2)}, u32[]{:S(2)}) collective-permute-start(bf16[2,96,768]{2,1,0:T(8,128)(2,1)S(1)} %fusion.40), channel_id=1, source_target_pairs={{0,0},{1,8},{2,16},{3,24},{4,1},{5,9},{6,17},{7,25},{8,2},{9,10},{... | collective-permute-start | bytes 884744 | tf_op jit(solution)/shard_map/ppermute | solution.py:139
  (57 other events, 186.7 us)
Sparse Core Ops, SparseCore 0:
  12.5 31.5 all-gather.6
  45.7 19.9 all-gather.4

commit v2 on v1

--- a/solution.py
+++ b/solution.py
@@ -110,21 +110,33 @@
         along_ref[head : head + 1, :] = jnp.sum(summed, axis=0, keepdims=True)
 
 
-def rep_reduce(blocks, order):
-    count = blocks.shape[0]
-    bits = count.bit_length() - 1
-    me = lax.axis_index("rep")
-    rest = blocks.shape[1:]
-    value = blocks.reshape((2,) * bits + rest)
-    left = list(range(bits - 1, -1, -1))
+def rep_blocks(blocks):
+    bits = blocks.shape[0].bit_length() - 1
+    return blocks.reshape((2,) * bits + blocks.shape[1:]), list(range(bits - 1, -1, -1))
+
+
+def rep_step(value, left, bit):
+    count = lax.axis_size("rep")
+    axis = left.index(bit)
+    mine = (lax.axis_index("rep") >> bit) & 1
+    send = lax.dynamic_index_in_dim(value, 1 - mine, axis, keepdims=False).astype(BF)
+    keep = lax.dynamic_index_in_dim(value, mine, axis, keepdims=False).astype(F32)
+    taken = lax.ppermute(send, "rep", [(i, i ^ (1 << bit)) for i in range(count)])
+    return keep + taken.astype(F32), [other for other in left if other != bit]
+
+
+def rep_reduce(value, left, order):
     for bit in order:
-        axis = left.index(bit)
-        mine = (me >> bit) & 1
-        send = lax.dynamic_index_in_dim(value, 1 - mine, axis, keepdims=False).astype(BF)
-        keep = lax.dynamic_index_in_dim(value, mine, axis, keepdims=False).astype(F32)
-        taken = lax.ppermute(send, "rep", [(i, i ^ (1 << bit)) for i in range(count)])
-        value = keep + taken.astype(F32)
-        left.remove(bit)
+        value, left = rep_step(value, left, bit)
+    return value
+
+
+def rep_sum(value):
+    count = lax.axis_size("rep")
+    bit = 1
+    while bit < count:
+        value = value + lax.ppermute(value, "rep", [(i, i ^ bit) for i in range(count)])
+        bit *= 2
     return value
 
 
@@ -179,18 +191,13 @@
             expert_ids[:, 0].astype(BF),
         ]
     )
-    small = jnp.pad(small, (0, 2 * D - small.shape[0]))[None]
-    pack = jnp.concatenate(
-        [
-            jnp.concatenate([tokens, cotangent], axis=1),
-            jnp.pad(small, ((0, 15), (0, 0))),
-        ],
-        axis=0,
-    )
-    got = lax.all_gather(pack, "fsdp")
-    x_all = got[:, :rows, :D].reshape(group, D)
-    g_all = got[:, :rows, D:].reshape(group, D).astype(F32)
-    sm = got[:, rows]
+    small = jnp.pad(small, (0, 2 * D - small.shape[0]))
+    small = small.reshape(2, D)
+    pack = jnp.concatenate([tokens, jnp.pad(small, ((0, 14), (0, 0)))], axis=0)
+    got = lax.all_gather(pack, "fsdp", axis=0, tiled=True).reshape(fc, rows + 16, D)
+    x_all = got[:, :rows].reshape(group, D)
+    g_all = lax.all_gather(cotangent, "fsdp", axis=0, tiled=True).astype(F32)
+    sm = got[:, rows : rows + 2].reshape(fc, 2 * D)
     gains = sm[:, :n_gain].reshape(fc, 2, width).transpose(1, 0, 2).reshape(2, D)
     at = n_gain
     table = sm[:, at : at + n_table].reshape(NB, H)
@@ -264,20 +271,21 @@
     sums = jnp.sum(parts.astype(F32), axis=0)
     routed, grad_hn = sums[:, :D], sums[:, D:]
 
-    def blocks_of(pieces, count):
+    def blocks_of(pieces):
         return jnp.stack(
             [piece.astype(BF).reshape(rc, piece.shape[0] // rc, piece.shape[1]) for piece in pieces],
             axis=1,
         )
 
-    in_share = rep_reduce(
-        blocks_of([product_tn(hn, u_zero), product_tn(hn, u_one)], rc), x_first
-    )
-    outer_share = rep_reduce(
-        blocks_of([product_tn(act_zero, grad_routed), product_tn(act_one, grad_routed)], rc),
-        z_first,
-    )
-    grad_w_out = to_owner(outer_share)
+    in_value, in_left = rep_step(
+        *rep_blocks(blocks_of([product_tn(hn, u_zero), product_tn(hn, u_one)])), x_first[0]
+    )
+    outer_value, outer_left = rep_step(
+        *rep_blocks(
+            blocks_of([product_tn(act_zero, grad_routed), product_tn(act_one, grad_routed)])
+        ),
+        z_first[0],
+    )
 
     hidden_own = own(hidden)
     hn_own = own(hn)
@@ -304,7 +312,14 @@
     branch_all = lax.all_gather(grad_hidden.astype(BF), "fsdp", axis=0, tiled=True)
     grad_attended = product_nt(branch_all, attn_out).astype(BF)
     out_part = product_tn(attended, branch_all).astype(BF)
-    out_share = to_owner(rep_reduce(out_part.reshape(rc, width // rc, D), x_first))
+    grad_attended, in_value, outer_value = lax.optimization_barrier(
+        (grad_attended, in_value, outer_value)
+    )
+    in_share = rep_reduce(in_value, in_left, x_first[1:])
+    grad_w_out = to_owner(rep_reduce(outer_value, outer_left, z_first[1:]))
+    out_share = to_owner(
+        rep_reduce(*rep_blocks(out_part.reshape(rc, width // rc, D)), x_first)
+    )
 
     grad_q, grad_k, grad_v, grad_along = pl.pallas_call(
         backward_kernel,
@@ -324,29 +339,9 @@
         product_nt(grad_q, qkv_cols[0])
         + product_nt(grad_k, qkv_cols[1])
         + product_nt(grad_v, qkv_cols[2])
-    ).astype(BF)
-    xn_parts = lax.all_to_all(xn_part.reshape(fc, rows, D), "fsdp", 0, 0, tiled=True)
-    grad_normed = jnp.sum(xn_parts.astype(F32), axis=0)
-
-    grad_stack = jnp.concatenate([grad_q, grad_k, grad_v], axis=1)
-    qkv_part = product_tn(normed, grad_stack).astype(BF)
-    qkv_share = rep_reduce(qkv_part.reshape(rc, D // rc, 3 * width), x_first)
-    piece = D // (rc * fc)
-    qkv_share = lax.all_to_all(
-        qkv_share.astype(BF).reshape(fc, piece, 3 * width), "fsdp", 0, 0, tiled=True
-    )
-    grad_qkv = (
-        qkv_share.astype(F32)
-        .reshape(fc, piece, 3, width)
-        .transpose(2, 1, 0, 3)
-        .reshape(3, piece, D)
-    )
-
+    )
     gain_one = gains[0].astype(F32)
-    grad_input_part, grad_gain_one = jax.vjp(norm_rows, tokens.astype(F32), gain_one)[1](
-        grad_normed
-    )
-    grad_tokens = grad_hidden + grad_input_part
+    grad_gain_one = jnp.sum(xn_part * norm_rows(inputs, jnp.ones((), F32)), axis=0)
     table_own_grad = lax.dot_general(
         codes.astype(F32),
         grad_along[:heads],
@@ -357,22 +352,47 @@
     table_grad = lax.dynamic_update_slice_in_dim(
         jnp.zeros((NB, H), F32), table_own_grad, f * heads, 1
     )
+    little = jnp.stack([grad_gain_one, grad_gain_two, grad_router[:, 0], grad_router[:, 1]])
     little = jnp.concatenate(
         [
-            grad_gain_one,
-            grad_gain_two,
-            grad_router.T.reshape(-1),
-            table_grad.reshape(-1),
-        ]
-    ).reshape(-1, 128)
-    little = lax.psum(little, ("rep", "fsdp")).reshape(-1)
-    grad_gains = lax.dynamic_slice_in_dim(little[: 2 * D].reshape(2, D), f * width, width, 1)
-    grad_router = lax.dynamic_slice_in_dim(
-        little[2 * D : 4 * D].reshape(EXPERTS, D), f * width, width, 1
-    ).T
-    grad_table = lax.dynamic_slice_in_dim(
-        little[4 * D :].reshape(NB, H), f * (NB // fc), NB // fc, 0
-    )
+            little.reshape(4, fc, width).transpose(1, 0, 2).reshape(fc, 4 * width),
+            table_grad.reshape(fc, NB // fc * H),
+        ],
+        axis=1,
+    )
+    n_little = little.shape[1]
+    high = little.astype(BF)
+    low = (little - high.astype(F32)).astype(BF)
+    little = jnp.pad(jnp.concatenate([high, low], axis=1), ((0, 0), (0, 3 * D - 2 * n_little)))
+    little = jnp.pad(little.reshape(fc, 3, D), ((0, 0), (0, 13), (0, 0)))
+    sent = jnp.concatenate([xn_part.astype(BF).reshape(fc, rows, D), little], axis=1)
+    xn_parts = lax.all_to_all(sent, "fsdp", 0, 0, tiled=True)
+    grad_normed = jnp.sum(xn_parts[:, :rows].astype(F32), axis=0)
+    little = jnp.sum(xn_parts[:, rows : rows + 3].astype(F32), axis=0).reshape(3 * D)
+    little = little[:n_little] + little[n_little : 2 * n_little]
+    little = rep_sum(jnp.pad(little, (0, 1024 - n_little)).reshape(8, 128)).reshape(-1)
+    grad_gains = little[: 2 * width].reshape(2, width)
+    grad_router = little[2 * width : 4 * width].reshape(EXPERTS, width).T
+    grad_table = little[4 * width : n_little].reshape(NB // fc, H)
+
+    grad_stack = jnp.concatenate([grad_q, grad_k, grad_v], axis=1)
+    qkv_part = product_tn(normed, grad_stack).astype(BF)
+    qkv_share = rep_reduce(*rep_blocks(qkv_part.reshape(rc, D // rc, 3 * width)), x_first)
+    piece = D // (rc * fc)
+    qkv_share = lax.all_to_all(
+        qkv_share.astype(BF).reshape(fc, piece, 3 * width), "fsdp", 0, 0, tiled=True
+    )
+    grad_qkv = (
+        qkv_share.astype(F32)
+        .reshape(fc, piece, 3, width)
+        .transpose(2, 1, 0, 3)
+        .reshape(3, piece, D)
+    )
+
+    grad_input_part = jax.vjp(lambda z: norm_rows(z, gain_one), tokens.astype(F32))[1](
+        grad_normed
+    )[0]
+    grad_tokens = grad_hidden + grad_input_part
     return (
         mixed,
         grad_tokens,

time: 308 us -> 254 us (0.82)
  waiting for transfers between devices: 82.1 us -> 44.2 us
  starting transfers between devices: 33 us -> 47.9 us
  local copies, waits for them, and re-layouts: 41.5 us -> 29.9 us
  blocking collectives: 64.3 us -> 54.3 us
  other arithmetic: 35.8 us -> 29.5 us
  matrix products: 26.7 us -> 22 us
    psum x1 -> x0, blocking collectives: 43.9 us -> none  [local(): little = lax.psum(little, ('rep', 'fsdp')).reshape(-1)]
    all_gather x0 -> x2, blocking collectives: none -> 35.6 us  [the longest x1 26.4 us: local(): lax.all_gather(pack, 'fsdp', axis=0, tiled=True).reshape(fc, rows + 16, D)]
    all_to_all x1, waiting for transfers between devices: 23.8 us -> 0.01 us  [local(): qkv_cols = lax.all_to_all(cut, 'fsdp', 0, 0, tiled=True)]
    ppermute x12 -> x15, waiting for transfers between devices: 32.9 us -> 21 us  [the longest x3 13.3 us: rep_sum(): lax.ppermute(value, 'rep', [(i, i ^ bit) for i in range(count)])]
    ppermute x12 -> x15, starting transfers between devices: 12.8 us -> 23.7 us  [the longest x12 17.7 us: rep_step(): taken = lax.ppermute(send, 'rep', [(i, i ^ 1 << bit) for i in range(count)])]
    unnamed x142 -> x77, local copies, waits for them, and re-layouts: 17.4 us -> 9.96 us
    add x9 -> x13, other arithmetic: 9.89 us -> 11.2 us  [the longest x9 10.3 us: rep_step(): return (keep + taken.astype(F32), [other for other in left if other != bit])]
  transfers between devices with their start and end apart: 20 -> 22, of which waited for: 7 -> 10; matrix products, arithmetic and copies ran while one was open for 20% -> 18% of each run, Pallas kernels for 3% -> 2%
where the time goes in v2:
time: 254 us; the launch traced here: 251 us
  blocking collectives  54.3 us (21%)
  starting transfers between devices  47.9 us (19%)
  waiting for transfers between devices  44.2 us (17%)
  local copies, waits for them, and re-layouts  29.9 us (12%)
  other arithmetic  29.5 us (12%)
  matrix products  22 us (9%)
  between operations  14.8 us (6%)
  Pallas kernels  8.01 us (3%)
    all_gather x1, blocking collectives, local(): lax.all_gather(pack, 'fsdp', axis=0, tiled=True).reshape(fc, rows + 16, D)  26.4 us
    ppermute x12, starting transfers between devices, rep_step(): taken = lax.ppermute(send, 'rep', [(i, i ^ 1 << bit) for i in range(count)])  17.7 us
    ppermute x2, waiting for transfers between devices, to_owner(): return lax.ppermute(value.astype(BF), ('rep', 'fsdp'), pairs).astype(F32)  13.4 us
    ppermute x3, waiting for transfers between devices, rep_sum(): lax.ppermute(value, 'rep', [(i, i ^ bit) for i in range(count)])  13.3 us
    all_gather x1, blocking collectives, local(): lax.all_gather(attended, 'fsdp').transpose(1, 0, 2).reshape(group, D)  10.8 us
    add x9, other arithmetic, rep_step(): return (keep + taken.astype(F32), [other for other in left if other != bit])  10.3 us
    unnamed x77, local copies, waits for them, and re-layouts  9.96 us
    all_gather x1, blocking collectives, local(): g_all = lax.all_gather(cotangent, 'fsdp', axis=0, tiled=True).astype(F32)  9.19 us
  transfers between devices with their start and end apart: 22, of which 10 were waited for; matrix products, arithmetic and copies ran while one was open for 18% of the time, Pallas kernels for 2%

profile of v2, /device:TPU:2, one launch (start us, length us, event | category | flops | bytes accessed | tf_op | source)
XLA Modules:
  0.0 250.7 jit_solution(14271644104221201037)
XLA Ops:
  7.2 2.9 %reshape.273 = bf16[3,192,4,192]{3,2,1,0:T(4,128)(2,1)S(1)} reshape(bf16[3,192,768]{2,1,0:T(8,128)(2,1)} %param.16) | data formatting | bytes 1769472 | tf_op jit(solution)/shard_map/reshape | solution.py:209
  11.3 3.7 %all-to-all-start = ((bf16[4,3,192,192]{3,2,1,0:T(8,128)(2,1)}), bf16[4,3,192,192]{3,2,1,0:T(8,128)(2,1)S(1)}, u32[]{:S(2)}, u32[]{:S(2)}) async-start(bf16[4,3,192,192]{3,2,1,0:T(8,128)(2,1)} %copy.77), calls=%async_computation | async-start | bytes 2359296 | tf_op jit(solution)/shard_map/all_to_all | solution.py:210
  16.4 26.4 %all_gather.18 = bf16[576,768]{1,0:T(8,128)(2,1)S(1)} all-gather(bf16[144,768]{1,0:T(8,128)(2,1)S(1)} %fusion.58), channel_id=1, replica_groups=mesh['rep'=8,'fsdp'=4] {'fsdp'}, dimensions={0}, use_global_device_ids=true | all-gather | bytes 1105920 | tf_op jit(solution)/shard_map/all_gather | solution.py:197
  45.5 9.2 %all_gather.22 = bf16[512,768]{1,0:T(8,128)(2,1)} all-gather(bf16[128,768]{1,0:T(8,128)(2,1)S(1)} %copy-done.14), channel_id=1, replica_groups=mesh['rep'=8,'fsdp'=4] {'fsdp'}, dimensions={0}, use_global_device_ids=true | all-gather | bytes 983040 | tf_op jit(solution)/shard_map/all_gather | solution.py:199
  55.8 4.1 %attention_forward.1 = (bf16[512,768]{1,0:T(8,128)(2,1)S(1)}, bf16[512,192]{1,0:T(8,128)(2,1)S(1)}, bf16[512,192]{1,0:T(8,128)(2,1)S(1)}, bf16[512,192]{1,0:T(8,...) custom-call(s32[1,2]{1,0:T(1,128)S(1)} %copy-done.2, bf16[512,768]{1,0:T(8,128)(2,1)S(1)} %bitcast.162, ...), custom_call_target="tpu_custom_call" | custom-call | tf_op jit(solution)/shard_map/attention_forward/pallas_call | solution.py:224
  61.5 10.8 %all-gather = bf16[2048,192]{1,0:T(8,128)(2,1)} all-gather(bf16[512,192]{1,0:T(8,128)(2,1)S(1)} %get-tuple-element.22), channel_id=2, replica_groups=mesh['rep'=8,'fsdp'=4] {'fsdp'}, dimensions={0}, use_global_device_ids=true | all-gather | bytes 983040 | tf_op jit(solution)/shard_map/all_gather | solution.py:240
  73.8 2.3 fusion.99
  76.1 2.2 multiply_reduce_fusion.1
  86.8 1.9 convolution_convert_fusion.3
  88.6 1.9 convolution_convert_fusion.2
  91.4 2.0 convolution_convert_fusion.1
  96.4 4.6 %all-to-all-start.1 = ((bf16[4,128,1536]{2,1,0:T(8,128)(2,1)}), bf16[4,128,1536]{2,1,0:T(8,128)(2,1)}, u32[]{:S(2)}, u32[]{:S(2)}) async-start(bf16[4,128,1536]{2,1,0:T(8,128)(2,1)} %bitcast.170), calls=%async_computation.1 | async-start | bytes 3145728 | tf_op jit(solution)/shard_map/all_to_all | solution.py:270
  101.0 2.9 %fusion.13 = (bf16[2,2,1,2,96,768]{5,4,2,1,0,3:T(8,128)(2,1)}, bf16[2,2,1,2,96,768]{5,4,2,1,0,3:T(8,128)(2,1)S(1)}) fusion(s32[]{:T(128)S(6)} %select_n.86, bf16[2,2,2,1,96,768]{5,4,2,1,0,3:T(8,128)(2,1)} %bitcast.181, bf16[2,2,2,1,96,768]{5,4,2,1,0,3:T(8,128)(2,1)} %bitcast.182, s32[]{:T(128)S(6)} %select_n.87), kind=kLoop, calls=%fused_computation.47 | loop fusion | flops 1179648 | bytes 4718600 | tf_op jit(solution)/shard_map/stack | solution.py:275
  111.7 9.2 %all-to-all-done.1 = bf16[4,128,1536]{2,1,0:T(8,128)(2,1)} async-done(((bf16[4,128,1536]{2,1,0:T(8,128)(2,1)}), bf16[4,128,1536]{2,1,0:T(8,128)(2,1)}, u32[]{:S(2)}, u32[]{:S(2)}) %all-to-all-start.1) | async-done | bytes 1572896 | tf_op jit(solution)/shard_map/all_to_all | solution.py:270
  120.9 1.9 convert_reduce_fusion
  124.8 8.0 %all_gather.23 = bf16[512,768]{1,0:T(8,128)(2,1)S(1)} all-gather(bf16[128,768]{1,0:T(8,128)(2,1)S(1)} %get-tuple-element.47), channel_id=1, replica_groups=mesh['rep'=8,'fsdp'=4] {'fsdp'}, dimensions={0}, use_global_device_ids=true | all-gather | bytes 983040 | tf_op jit(solution)/shard_map/all_gather | solution.py:312
  134.1 3.1 %convert_add_fusion.1 = f32[2,2,2,96,768]{4,3,2,0,1:T(8,128)} fusion(bf16[2,2,2,96,768]{4,3,2,0,1:T(8,128)(2,1)} %collective-permute-done, bf16[2,2,1,2,96,768]{5,4,2,1,0,3:T(8,128)(2,1)S(1)} %copy-done.8), kind=kLoop, calls=%fused_computation.10 | loop fusion | flops 1769472 | bytes 4718592 | tf_op jit(solution)/shard_map/add | solution.py:125
  137.6 3.1 %convert_add_fusion = f32[2,2,2,96,768]{4,3,2,0,1:T(8,128)} fusion(bf16[2,2,2,96,768]{4,3,2,0,1:T(8,128)(2,1)} %collective-permute-done.1, bf16[2,1,2,2,96,768]{5,4,2,1,0,3:T(8,128)(2,1)S(1)} %copy-done.9), kind=kLoop, calls=%fused_computation.9 | loop fusion | flops 1769472 | bytes 4718592 | tf_op jit(solution)/shard_map/add | solution.py:125
  140.6 3.9 %attention_backward.1 = (bf16[512,192]{1,0:T(8,128)(2,1)S(1)}, bf16[512,192]{1,0:T(8,128)(2,1)S(1)}, bf16[512,192]{1,0:T(8,128)(2,1)S(1)}, f32[8,1024]{1,0:T(8,128)S(1)}) custom-call(bf16[512,192]{1,0:T(8,128)(2,1)S(1)} %get-tuple-element.23.q_ref, bf16[512,192]{1,0:T(8,128)(2,1)S(1)} %get-tuple-element.24.k_ref, ...), custom_call_target="tpu_custom_call" | custom-call | tf_op jit(solution)/shard_map/attention_backward/pallas_call | solution.py:324
  148.9 4.2 %all-to-all-start.2 = ((bf16[4,144,768]{2,1,0:T(8,128)(2,1)}), bf16[4,144,768]{2,1,0:T(8,128)(2,1)}, u32[]{:S(2)}, u32[]{:S(2)}) async-start(bf16[4,144,768]{2,1,0:T(8,128)(2,1)} %fusion.34), calls=%async_computation.2 | async-start | bytes 1769472 | tf_op jit(solution)/shard_map/all_to_all | solution.py:369
  159.0 2.0 collective-permute-done.5
  166.5 2.6 %collective-permute-start.7 = (bf16[24,768]{1,0:T(8,128)(2,1)S(1)}, bf16[24,768]{1,0:T(8,128)(2,1)S(1)}, u32[]{:S(2)}, u32[]{:S(2)}) collective-permute-start(bf16[24,768]{1,0:T(8,128)(2,1)S(1)} %fusion.64), channel_id=1, source_target_pairs={{0,16},{4,20},{8,24},{12,28},{16,0},{20,4},{24,8},{28,12},{1,17},{... | collective-permute-start | bytes 110600 | tf_op jit(solution)/shard_map/ppermute | solution.py:124
  171.6 2.2 collective-permute-start.8
  173.9 5.7 %collective-permute-done.8 = bf16[24,768]{1,0:T(8,128)(2,1)S(1)} collective-permute-done((bf16[24,768]{1,0:T(8,128)(2,1)S(1)}, bf16[24,768]{1,0:T(8,128)(2,1)S(1)}, u32[]{:S(2)}, u32[]{:S(2)}) %collective-permute-start.8) | collective-permute-done | bytes 36896 | tf_op jit(solution)/shard_map/ppermute | solution.py:151
  181.2 4.7 %collective-permute-start.3 = (bf16[2,96,576]{2,1,0:T(8,128)(2,1)}, bf16[2,96,576]{2,1,0:T(8,128)(2,1)}, u32[]{:S(2)}, u32[]{:S(2)}) collective-permute-start(bf16[2,96,576]{2,1,0:T(8,128)(2,1)} %fusion.56), channel_id=1, source_target_pairs={{0,8},{4,12},{8,0},{12,4},{16,24},{20,28},{24,16},{28,20},{1,9},{5... | collective-permute-start | bytes 663560 | tf_op jit(solution)/shard_map/ppermute | solution.py:124
  187.7 3.0 %collective-permute-done.14 = bf16[2,2,96,768]{3,2,1,0:T(8,128)(2,1)S(1)} collective-permute-done((bf16[2,2,96,768]{3,2,1,0:T(8,128)(2,1)S(1)}, bf16[2,2,96,768]{3,2,1,0:T(8,128)(2,1)S(1)}, u32[]{:S(2)}, u32[]{:S(2)}) %collective-permute-start.14) | collective-permute-done | bytes 589856 | tf_op jit(solution)/shard_map/ppermute | solution.py:124
  199.8 2.6 %collective-permute-start.10 = (f32[8,128]{1,0:T(8,128)S(1)}, f32[8,128]{1,0:T(8,128)S(1)}, u32[]{:S(2)}, u32[]{:S(2)}) collective-permute-start(f32[8,128]{1,0:T(8,128)S(1)} %fusion.95), channel_id=1, source_target_pairs={{0,8},{4,12},{8,0},{12,4},{16,24},{20,28},{24,16},{28,20},{1,9},{5... | collective-permute-start | bytes 12296 | tf_op jit(solution)/shard_map/ppermute | solution.py:138
  206.5 12.3 %collective-permute-done.11 = f32[8,128]{1,0:T(8,128)S(1)} collective-permute-done((f32[8,128]{1,0:T(8,128)S(1)}, f32[8,128]{1,0:T(8,128)S(1)}, u32[]{:S(2)}, u32[]{:S(2)}) %collective-permute-start.11) | collective-permute-done | bytes 4128 | tf_op jit(solution)/shard_map/ppermute | solution.py:138
  219.5 5.2 %all-to-all-start.3 = ((bf16[4,24,576]{2,1,0:T(8,128)(2,1)}), bf16[4,24,576]{2,1,0:T(8,128)(2,1)S(1)}, u32[]{:S(2)}, u32[]{:S(2)}) async-start(bf16[4,24,576]{2,1,0:T(8,128)(2,1)} %bitcast.41), calls=%async_computation.3 | async-start | bytes 245760 | tf_op jit(solution)/shard_map/all_to_all | solution.py:382
  225.7 4.4 %collective-permute-start.16 = (bf16[2,96,768]{2,1,0:T(8,128)(2,1)S(1)}, bf16[2,96,768]{2,1,0:T(8,128)(2,1)S(1)}, u32[]{:S(2)}, u32[]{:S(2)}) collective-permute-start(bf16[2,96,768]{2,1,0:T(8,128)(2,1)S(1)} %fusion.42), channel_id=1, source_target_pairs={{0,0},{1,8},{2,16},{3,24},{4,1},{5,9},{6,17},{7,25},{8,2},{9,10},{... | collective-permute-start | bytes 884744 | tf_op jit(solution)/shard_map/ppermute | solution.py:151
  233.5 1.8 bitcast_add_fusion.3
  235.3 7.7 %collective-permute-done.16 = bf16[2,96,768]{2,1,0:T(8,128)(2,1)S(1)} collective-permute-done((bf16[2,96,768]{2,1,0:T(8,128)(2,1)S(1)}, bf16[2,96,768]{2,1,0:T(8,128)(2,1)S(1)}, u32[]{:S(2)}, u32[]{:S(2)}) %collective-permute-start.16) | collective-permute-done | bytes 294944 | tf_op jit(solution)/shard_map/ppermute | solution.py:151
  (232 shorter events, 73.6 us)
Async XLA Ops:
  11.3 43.4 %all-to-all-start = ((bf16[4,3,192,192]{3,2,1,0:T(8,128)(2,1)}), bf16[4,3,192,192]{3,2,1,0:T(8,128)(2,1)S(1)}, u32[]{:S(2)}, u32[]{:S(2)}) async-start(bf16[4,3,192,192]{3,2,1,0:T(8,128)(2,1)} %copy.77), calls=%async_computation | async-start | bytes 2359296 | tf_op jit(solution)/shard_map/all_to_all | solution.py:210
  14.9 28.4 %copy-start.26 = (s32[1023]{0:T(1024)S(1)}, s32[1023]{0:T(1024)}, u32[]{:S(2)}) copy-start(s32[1023]{0:T(1024)} %param.15) | copy-start | bytes 12280
  15.0 61.1 %all-gather.3.cloned.1.call-start = ((), (), s32[]{:S(2)}) async-start(), calls=%async_computation.4 | async-start | bytes 1474560 | tf_op jit(solution)/shard_map/all_gather | solution.py:212
  45.5 10.3 %copy-start.2 = (s32[1,2]{1,0:T(1,128)S(1)}, s32[1,2]{1,0:T(1,128)}, u32[]{:S(2)}) copy-start(s32[1,2]{1,0:T(1,128)} %lengths.1) | copy-start | bytes 28
  83.5 10.8 %copy-start.33 = (bf16[512,768]{1,0:T(8,128)(2,1)}, bf16[512,768]{1,0:T(8,128)(2,1)S(1)}, u32[]{:S(2)}) copy-start(bf16[512,768]{1,0:T(8,128)(2,1)S(1)} %get-tuple-element.73) | copy-start | bytes 2359300
  96.4 24.5 %all-to-all-start.1 = ((bf16[4,128,1536]{2,1,0:T(8,128)(2,1)}), bf16[4,128,1536]{2,1,0:T(8,128)(2,1)}, u32[]{:S(2)}, u32[]{:S(2)}) async-start(bf16[4,128,1536]{2,1,0:T(8,128)(2,1)} %bitcast.170), calls=%async_computation.1 | async-start | bytes 3145728 | tf_op jit(solution)/shard_map/all_to_all | solution.py:270
  105.0 28.6 %collective-permute-start = (bf16[2,2,2,96,768]{4,3,2,0,1:T(8,128)(2,1)}, bf16[2,2,2,96,768]{4,3,2,0,1:T(8,128)(2,1)}, u32[]{:S(2)}, u32[]{:S(2)}) collective-permute-start(bf16[2,2,2,96,768]{4,3,2,0,1:T(8,128)(2,1)} %bitcast.160), channel_id=1, source_target_pairs={{0,4},{4,0},{8,12},{12,8},{16,20},{20,16},{24,28},{28,24},{1,5},{5... | collective-permute-start | bytes 3538952 | tf_op jit(solution)/shard_map/ppermute | solution.py:124
  109.0 28.5 %collective-permute-start.1 = (bf16[2,2,2,96,768]{4,3,2,0,1:T(8,128)(2,1)}, bf16[2,2,2,96,768]{4,3,2,0,1:T(8,128)(2,1)}, u32[]{:S(2)}, u32[]{:S(2)}) collective-permute-start(bf16[2,2,2,96,768]{4,3,2,0,1:T(8,128)(2,1)} %bitcast.159), channel_id=1, source_target_pairs={{0,8},{4,12},{8,0},{12,4},{16,24},{20,28},{24,16},{28,20},{1,9},{5... | collective-permute-start | bytes 3538952 | tf_op jit(solution)/shard_map/ppermute | solution.py:124
  123.5 9.3 %copy-start.25 = (bf16[192,768]{1,0:T(8,128)(2,1)S(1)}, bf16[192,768]{1,0:T(8,128)(2,1)}, u32[]{:S(2)}) copy-start(bf16[192,768]{1,0:T(8,128)(2,1)} %param.17) | copy-start | bytes 884740
  148.9 44.3 %all-to-all-start.2 = ((bf16[4,144,768]{2,1,0:T(8,128)(2,1)}), bf16[4,144,768]{2,1,0:T(8,128)(2,1)}, u32[]{:S(2)}, u32[]{:S(2)}) async-start(bf16[4,144,768]{2,1,0:T(8,128)(2,1)} %fusion.34), calls=%async_computation.2 | async-start | bytes 1769472 | tf_op jit(solution)/shard_map/all_to_all | solution.py:369
  154.5 6.5 %collective-permute-start.5 = (bf16[2,2,24,768]{3,2,0,1:T(8,128)(2,1)}, bf16[2,2,24,768]{3,2,0,1:T(8,128)(2,1)}, u32[]{:S(2)}, u32[]{:S(2)}) collective-permute-start(bf16[2,2,24,768]{3,2,0,1:T(8,128)(2,1)} %bitcast.161), channel_id=1, source_target_pairs={{0,4},{4,0},{8,12},{12,8},{16,20},{20,16},{24,28},{28,24},{1,5},{5... | collective-permute-start | bytes 442376 | tf_op jit(solution)/shard_map/ppermute | solution.py:124
  157.3 11.9 %copy-start.5 = (f32[2,2,2,96,768]{4,3,2,0,1:T(8,128)S(1)}, f32[2,2,2,96,768]{4,3,2,0,1:T(8,128)}, u32[]{:S(2)}) copy-start(f32[2,2,2,96,768]{4,3,2,0,1:T(8,128)} %convert_add_fusion.1) | copy-start | bytes 7077892
  162.0 11.7 %copy-start.4 = (f32[2,2,2,96,768]{4,3,2,0,1:T(8,128)S(1)}, f32[2,2,2,96,768]{4,3,2,0,1:T(8,128)}, u32[]{:S(2)}) copy-start(f32[2,2,2,96,768]{4,3,2,0,1:T(8,128)} %convert_add_fusion) | copy-start | bytes 7077892
  162.1 4.4 %collective-permute-start.6 = (bf16[2,24,768]{2,1,0:T(8,128)(2,1)S(1)}, bf16[2,24,768]{2,1,0:T(8,128)(2,1)S(1)}, u32[]{:S(2)}, u32[]{:S(2)}) collective-permute-start(bf16[2,24,768]{2,1,0:T(8,128)(2,1)S(1)} %fusion.62), channel_id=1, source_target_pairs={{0,8},{4,12},{8,0},{12,4},{16,24},{20,28},{24,16},{28,20},{1,9},{5... | collective-permute-start | bytes 221192 | tf_op jit(solution)/shard_map/ppermute | solution.py:124
  163.7 16.5 %collective-permute-start.2 = (bf16[2,2,96,576]{3,2,1,0:T(8,128)(2,1)S(1)}, bf16[2,2,96,576]{3,2,1,0:T(8,128)(2,1)S(1)}, u32[]{:S(2)}, u32[]{:S(2)}) collective-permute-start(bf16[2,2,96,576]{3,2,1,0:T(8,128)(2,1)S(1)} %dynamic-slice_bitcast_fusion), channel_id=1, source_target_pairs={{0,4},{4,0},{8,12},{12,8},{16,20},{20,16},{24,28},{28,24},{1,5},{5... | collective-permute-start | bytes 1327112 | tf_op jit(solution)/shard_map/ppermute | solution.py:124
  166.5 5.0 %collective-permute-start.7 = (bf16[24,768]{1,0:T(8,128)(2,1)S(1)}, bf16[24,768]{1,0:T(8,128)(2,1)S(1)}, u32[]{:S(2)}, u32[]{:S(2)}) collective-permute-start(bf16[24,768]{1,0:T(8,128)(2,1)S(1)} %fusion.64), channel_id=1, source_target_pairs={{0,16},{4,20},{8,24},{12,28},{16,0},{20,4},{24,8},{28,12},{1,17},{... | collective-permute-start | bytes 110600 | tf_op jit(solution)/shard_map/ppermute | solution.py:124
  169.2 16.7 %collective-permute-start.12 = (bf16[2,2,96,768]{3,2,1,0:T(8,128)(2,1)S(1)}, bf16[2,2,96,768]{3,2,1,0:T(8,128)(2,1)S(1)}, u32[]{:S(2)}, u32[]{:S(2)}) collective-permute-start(bf16[2,2,96,768]{3,2,1,0:T(8,128)(2,1)S(1)} %fusion.40), channel_id=1, source_target_pairs={{0,8},{4,12},{8,0},{12,4},{16,24},{20,28},{24,16},{28,20},{1,9},{5... | collective-permute-start | bytes 1769480 | tf_op jit(solution)/shard_map/ppermute | solution.py:124
  171.6 8.0 %collective-permute-start.8 = (bf16[24,768]{1,0:T(8,128)(2,1)S(1)}, bf16[24,768]{1,0:T(8,128)(2,1)S(1)}, u32[]{:S(2)}, u32[]{:S(2)}) collective-permute-start(bf16[24,768]{1,0:T(8,128)(2,1)S(1)} %fusion.63), channel_id=1, source_target_pairs={{0,0},{1,8},{2,16},{3,24},{4,1},{5,9},{6,17},{7,25},{8,2},{9,10},{... | collective-permute-start | bytes 110600 | tf_op jit(solution)/shard_map/ppermute | solution.py:151
  173.8 16.8 %collective-permute-start.14 = (bf16[2,2,96,768]{3,2,1,0:T(8,128)(2,1)S(1)}, bf16[2,2,96,768]{3,2,1,0:T(8,128)(2,1)S(1)}, u32[]{:S(2)}, u32[]{:S(2)}) collective-permute-start(bf16[2,2,96,768]{3,2,1,0:T(8,128)(2,1)S(1)} %fusion.41), channel_id=1, source_target_pairs={{0,4},{4,0},{8,12},{12,8},{16,20},{20,16},{24,28},{28,24},{1,5},{5... | collective-permute-start | bytes 1769480 | tf_op jit(solution)/shard_map/ppermute | solution.py:124
  180.3 5.5 %copy-start.10 = (f32[2,2,96,576]{3,2,1,0:T(8,128)}, f32[2,2,96,576]{3,2,1,0:T(8,128)S(1)}, u32[]{:S(2)}) copy-start(f32[2,2,96,576]{3,2,1,0:T(8,128)S(1)} %convert_add_fusion.3) | copy-start | bytes 2654212
  181.2 17.6 %collective-permute-start.3 = (bf16[2,96,576]{2,1,0:T(8,128)(2,1)}, bf16[2,96,576]{2,1,0:T(8,128)(2,1)}, u32[]{:S(2)}, u32[]{:S(2)}) collective-permute-start(bf16[2,96,576]{2,1,0:T(8,128)(2,1)} %fusion.56), channel_id=1, source_target_pairs={{0,8},{4,12},{8,0},{12,4},{16,24},{20,28},{24,16},{28,20},{1,9},{5... | collective-permute-start | bytes 663560 | tf_op jit(solution)/shard_map/ppermute | solution.py:124
  186.7 46.7 %collective-permute-start.13 = (bf16[2,96,768]{2,1,0:T(8,128)(2,1)}, bf16[2,96,768]{2,1,0:T(8,128)(2,1)}, u32[]{:S(2)}, u32[]{:S(2)}) collective-permute-start(bf16[2,96,768]{2,1,0:T(8,128)(2,1)} %fusion.50), channel_id=1, source_target_pairs={{0,16},{4,20},{8,24},{12,28},{16,0},{20,4},{24,8},{28,12},{1,17},{... | collective-permute-start | bytes 884744 | tf_op jit(solution)/shard_map/ppermute | solution.py:124
  190.8 7.8 %copy-start.13 = (bf16[128,768]{1,0:T(8,128)(2,1)S(1)}, bf16[128,768]{1,0:T(8,128)(2,1)}, u32[]{:S(2)}) copy-start(bf16[128,768]{1,0:T(8,128)(2,1)} %param.12) | copy-start | bytes 589828
  190.8 8.0 %copy-start.11 = (f32[2,2,96,576]{3,2,1,0:T(8,128)S(1)}, f32[2,2,96,576]{3,2,1,0:T(8,128)}, u32[]{:S(2)}) copy-start(f32[2,2,96,576]{3,2,1,0:T(8,128)} %copy-done.10) | copy-start | bytes 2654212
  191.5 33.2 %collective-permute-start.15 = (bf16[2,96,768]{2,1,0:T(8,128)(2,1)}, bf16[2,96,768]{2,1,0:T(8,128)(2,1)}, u32[]{:S(2)}, u32[]{:S(2)}) collective-permute-start(bf16[2,96,768]{2,1,0:T(8,128)(2,1)} %fusion.51), channel_id=1, source_target_pairs={{0,16},{4,20},{8,24},{12,28},{16,0},{20,4},{24,8},{28,12},{1,17},{... | collective-permute-start | bytes 884744 | tf_op jit(solution)/shard_map/ppermute | solution.py:124
  195.5 10.1 %copy-start.19 = (f32[128,768]{1,0:T(8,128)S(1)}, f32[128,768]{1,0:T(8,128)}, u32[]{:S(2)}) copy-start(f32[128,768]{1,0:T(8,128)} %get-tuple-element.48) | copy-start | bytes 1179652
  195.5 4.3 %collective-permute-start.9 = (f32[8,128]{1,0:T(8,128)S(1)}, f32[8,128]{1,0:T(8,128)S(1)}, u32[]{:S(2)}, u32[]{:S(2)}) collective-permute-start(f32[8,128]{1,0:T(8,128)S(1)} %pad_bitcast_fusion), channel_id=1, source_target_pairs={{0,4},{4,0},{8,12},{12,8},{16,20},{20,16},{24,28},{28,24},{1,5},{5... | collective-permute-start | bytes 12296 | tf_op jit(solution)/shard_map/ppermute | solution.py:138
  199.8 4.2 %collective-permute-start.10 = (f32[8,128]{1,0:T(8,128)S(1)}, f32[8,128]{1,0:T(8,128)S(1)}, u32[]{:S(2)}, u32[]{:S(2)}) collective-permute-start(f32[8,128]{1,0:T(8,128)S(1)} %fusion.95), channel_id=1, source_target_pairs={{0,8},{4,12},{8,0},{12,4},{16,24},{20,28},{24,16},{28,20},{1,9},{5... | collective-permute-start | bytes 12296 | tf_op jit(solution)/shard_map/ppermute | solution.py:138
  202.4 16.4 %collective-permute-start.4 = (bf16[96,576]{1,0:T(8,128)(2,1)S(1)}, bf16[96,576]{1,0:T(8,128)(2,1)S(1)}, u32[]{:S(2)}, u32[]{:S(2)}) collective-permute-start(bf16[96,576]{1,0:T(8,128)(2,1)S(1)} %fusion.61), channel_id=1, source_target_pairs={{0,16},{4,20},{8,24},{12,28},{16,0},{20,4},{24,8},{28,12},{1,17},{... | collective-permute-start | bytes 331784 | tf_op jit(solution)/shard_map/ppermute | solution.py:124
  204.0 14.8 %collective-permute-start.11 = (f32[8,128]{1,0:T(8,128)S(1)}, f32[8,128]{1,0:T(8,128)S(1)}, u32[]{:S(2)}, u32[]{:S(2)}) collective-permute-start(f32[8,128]{1,0:T(8,128)S(1)} %fusion.125), channel_id=1, source_target_pairs={{0,16},{4,20},{8,24},{12,28},{16,0},{20,4},{24,8},{28,12},{1,17},{... | collective-permute-start | bytes 12296 | tf_op jit(solution)/shard_map/ppermute | solution.py:138
  219.5 12.6 %all-to-all-start.3 = ((bf16[4,24,576]{2,1,0:T(8,128)(2,1)}), bf16[4,24,576]{2,1,0:T(8,128)(2,1)S(1)}, u32[]{:S(2)}, u32[]{:S(2)}) async-start(bf16[4,24,576]{2,1,0:T(8,128)(2,1)} %bitcast.41), calls=%async_computation.3 | async-start | bytes 245760 | tf_op jit(solution)/shard_map/all_to_all | solution.py:382
  225.7 17.3 %collective-permute-start.16 = (bf16[2,96,768]{2,1,0:T(8,128)(2,1)S(1)}, bf16[2,96,768]{2,1,0:T(8,128)(2,1)S(1)}, u32[]{:S(2)}, u32[]{:S(2)}) collective-permute-start(bf16[2,96,768]{2,1,0:T(8,128)(2,1)S(1)} %fusion.42), channel_id=1, source_target_pairs={{0,0},{1,8},{2,16},{3,24},{4,1},{5,9},{6,17},{7,25},{8,2},{9,10},{... | collective-permute-start | bytes 884744 | tf_op jit(solution)/shard_map/ppermute | solution.py:151
  (25 other events, 59.5 us)
Sparse Core Ops, SparseCore 0:
  17.4 25.5 all-gather.2

commit v3 on v2

--- a/solution.py
+++ b/solution.py
@@ -196,7 +196,9 @@
     pack = jnp.concatenate([tokens, jnp.pad(small, ((0, 14), (0, 0)))], axis=0)
     got = lax.all_gather(pack, "fsdp", axis=0, tiled=True).reshape(fc, rows + 16, D)
     x_all = got[:, :rows].reshape(group, D)
-    g_all = lax.all_gather(cotangent, "fsdp", axis=0, tiled=True).astype(F32)
+    later = lax.all_gather(jnp.concatenate([attn_out, cotangent], axis=0), "fsdp")
+    out_full = later[:, :width].reshape(D, D)
+    g_all = later[:, width:].reshape(group, D).astype(F32)
     sm = got[:, rows : rows + 2].reshape(fc, 2 * D)
     gains = sm[:, :n_gain].reshape(fc, 2, width).transpose(1, 0, 2).reshape(2, D)
     at = n_gain
@@ -209,7 +211,6 @@
     cut = attn_qkv.reshape(3, width, fc, width).transpose(2, 0, 1, 3)
     qkv_cols = lax.all_to_all(cut, "fsdp", 0, 0, tiled=True)
     qkv_cols = qkv_cols.transpose(1, 0, 2, 3).reshape(3, D, width)
-    out_full = lax.all_gather(attn_out, "fsdp", axis=0, tiled=True)
 
     codes = (
         jnp.pad(rel_buckets, (0, 1))[:, None] == jnp.arange(NB, dtype=jnp.int32)[None, :]
@@ -267,6 +268,9 @@
     u_one = jnp.where(first, none, grad_u)
     hn_part = product_nt(u_zero, w_in[0]) + product_nt(u_one, w_in[1])
     parts = jnp.concatenate([routed_part.astype(BF), hn_part.astype(BF)], axis=1)
+    parts, u_zero, u_one, act_zero, act_one = lax.optimization_barrier(
+        (parts, u_zero, u_one, act_zero, act_one)
+    )
     parts = lax.all_to_all(parts.reshape(fc, rows, 2 * D), "fsdp", 0, 0, tiled=True)
     sums = jnp.sum(parts.astype(F32), axis=0)
     routed, grad_hn = sums[:, :D], sums[:, D:]
@@ -315,8 +319,8 @@
     grad_attended, in_value, outer_value = lax.optimization_barrier(
         (grad_attended, in_value, outer_value)
     )
-    in_share = rep_reduce(in_value, in_left, x_first[1:])
-    grad_w_out = to_owner(rep_reduce(outer_value, outer_left, z_first[1:]))
+    in_value, in_left = rep_step(in_value, in_left, x_first[1])
+    outer_value, outer_left = rep_step(outer_value, outer_left, z_first[1])
     out_share = to_owner(
         rep_reduce(*rep_blocks(out_part.reshape(rc, width // rc, D)), x_first)
     )
@@ -332,6 +336,11 @@
             jax.ShapeDtypeStruct((8, span), F32),
         ],
         compiler_params=pltpu.CompilerParams(vmem_limit_bytes=40 << 20),
+        cost_estimate=pl.CostEstimate(
+            flops=10 * heads * group * group * HD,
+            bytes_accessed=16 * heads * group * group,
+            transcendentals=0,
+        ),
         name="attention_backward",
     )(queries, keys, values, probs, grad_attended)
 
@@ -367,6 +376,16 @@
     little = jnp.pad(little.reshape(fc, 3, D), ((0, 0), (0, 13), (0, 0)))
     sent = jnp.concatenate([xn_part.astype(BF).reshape(fc, rows, D), little], axis=1)
     xn_parts = lax.all_to_all(sent, "fsdp", 0, 0, tiled=True)
+    grad_stack = jnp.concatenate([grad_q, grad_k, grad_v], axis=1)
+    qkv_part = product_tn(normed, grad_stack).astype(BF)
+    qkv_part, in_value, outer_value = lax.optimization_barrier((qkv_part, in_value, outer_value))
+    in_share = rep_reduce(in_value, in_left, x_first[2:])
+    grad_w_out = to_owner(rep_reduce(outer_value, outer_left, z_first[2:]))
+    qkv_value, qkv_left = rep_step(
+        *rep_blocks(qkv_part.reshape(rc, D // rc, 3 * width)), x_first[0]
+    )
+    qkv_value, xn_parts = lax.optimization_barrier((qkv_value, xn_parts))
+    qkv_share = rep_reduce(qkv_value, qkv_left, x_first[1:])
     grad_normed = jnp.sum(xn_parts[:, :rows].astype(F32), axis=0)
     little = jnp.sum(xn_parts[:, rows : rows + 3].astype(F32), axis=0).reshape(3 * D)
     little = little[:n_little] + little[n_little : 2 * n_little]
@@ -375,9 +394,6 @@
     grad_router = little[2 * width : 4 * width].reshape(EXPERTS, width).T
     grad_table = little[4 * width : n_little].reshape(NB // fc, H)
 
-    grad_stack = jnp.concatenate([grad_q, grad_k, grad_v], axis=1)
-    qkv_part = product_tn(normed, grad_stack).astype(BF)
-    qkv_share = rep_reduce(*rep_blocks(qkv_part.reshape(rc, D // rc, 3 * width)), x_first)
     piece = D // (rc * fc)
     qkv_share = lax.all_to_all(
         qkv_share.astype(BF).reshape(fc, piece, 3 * width), "fsdp", 0, 0, tiled=True

time: 254 us -> 250 us (0.984)
  starting transfers between devices: 47.9 us -> 40.6 us
  other arithmetic: 29.5 us -> 34.9 us
  blocking collectives: 54.3 us -> 50.4 us
  waiting for transfers between devices: 44.2 us -> 47.4 us
  matrix products: 22 us -> 19.2 us
    ppermute x12, waiting for transfers between devices: 7.7 us -> 28.2 us  [rep_step(): taken = lax.ppermute(send, 'rep', [(i, i ^ 1 << bit) for i in range(count)])]
    ppermute x2, waiting for transfers between devices: 13.4 us -> 0.01 us  [to_owner(): return lax.ppermute(value.astype(BF), ('rep', 'fsdp'), pairs).astype(F32)]
    all_gather x1 -> x0, blocking collectives: 9.19 us -> none  [local(): g_all = lax.all_gather(cotangent, 'fsdp', axis=0, tiled=True).astype(F32)]
    ppermute x3, starting transfers between devices: 6.01 us -> 0.61 us  [rep_sum(): lax.ppermute(value, 'rep', [(i, i ^ bit) for i in range(count)])]
    all_gather x1, blocking collectives: 26.4 us -> 31.3 us  [local(): lax.all_gather(pack, 'fsdp', axis=0, tiled=True).reshape(fc, rows + 16, D)]
    convert_element_type x8, local copies, waits for them, and re-layouts: 2.48 us -> 5.23 us  [rep_step(): lax.dynamic_index_in_dim(value, 1 - mine, axis, keepdims=False).astype(BF)]
    convert_element_type x0 -> x3, other arithmetic: none -> 2.71 us  [the longest x1 1.41 us: local(): g_all = later[:, width:].reshape(group, D).astype(F32)]
    unnamed x77 -> x91, local copies, waits for them, and re-layouts: 9.96 us -> 10.3 us
  transfers between devices with their start and end apart: 22 -> 22, of which waited for: 10 -> 11; matrix products, arithmetic and copies ran while one was open for 18% -> 24% of each run, Pallas kernels for 2% -> 3%
where the time goes in v3:
time: 250 us; the launch traced here: 246 us
  blocking collectives  50.4 us (20%)
  waiting for transfers between devices  47.4 us (19%)
  starting transfers between devices  40.6 us (16%)
  other arithmetic  34.9 us (14%)
  local copies, waits for them, and re-layouts  30.2 us (12%)
  matrix products  19.2 us (8%)
  between operations  15 us (6%)
  Pallas kernels  8.01 us (3%)
    all_gather x1, blocking collectives, local(): lax.all_gather(pack, 'fsdp', axis=0, tiled=True).reshape(fc, rows + 16, D)  31.3 us
    ppermute x12, waiting for transfers between devices, rep_step(): taken = lax.ppermute(send, 'rep', [(i, i ^ 1 << bit) for i in range(count)])  28.2 us
    ppermute x12, starting transfers between devices, rep_step(): taken = lax.ppermute(send, 'rep', [(i, i ^ 1 << bit) for i in range(count)])  17.9 us
    ppermute x3, waiting for transfers between devices, rep_sum(): lax.ppermute(value, 'rep', [(i, i ^ bit) for i in range(count)])  10.9 us
    all_gather x1, blocking collectives, local(): lax.all_gather(attended, 'fsdp').transpose(1, 0, 2).reshape(group, D)  10.8 us
    add x9, other arithmetic, rep_step(): return (keep + taken.astype(F32), [other for other in left if other != bit])  10.6 us
    unnamed x91, local copies, waits for them, and re-layouts  10.3 us
    all_gather x1, blocking collectives, local(): lax.all_gather(grad_hidden.astype(BF), 'fsdp', axis=0, tiled=True)  8.35 us
  transfers between devices with their start and end apart: 22, of which 11 were waited for; matrix products, arithmetic and copies ran while one was open for 24% of the time, Pallas kernels for 3%

profile of v3, /device:TPU:2, one launch (start us, length us, event | category | flops | bytes accessed | tf_op | source)
XLA Modules:
  0.0 245.7 jit_solution(9035526799351382502)
XLA Ops:
  7.2 1.9 pad_maximum_fusion.1
  11.4 3.7 %all-to-all-start = ((bf16[4,3,192,192]{3,2,1,0:T(8,128)(2,1)}), bf16[4,3,192,192]{3,2,1,0:T(8,128)(2,1)S(1)}, u32[]{:S(2)}, u32[]{:S(2)}) async-start(bf16[4,3,192,192]{3,2,1,0:T(8,128)(2,1)} %copy.78), calls=%async_computation | async-start | bytes 2359296 | tf_op jit(solution)/shard_map/all_to_all | solution.py:212
  15.8 31.3 %all_gather.18 = bf16[576,768]{1,0:T(8,128)(2,1)S(1)} all-gather(bf16[144,768]{1,0:T(8,128)(2,1)S(1)} %fusion.61), channel_id=1, replica_groups=mesh['rep'=8,'fsdp'=4] {'fsdp'}, dimensions={0}, use_global_device_ids=true | all-gather | bytes 1105920 | tf_op jit(solution)/shard_map/all_gather | solution.py:197
  51.7 4.1 %attention_forward.1 = (bf16[512,768]{1,0:T(8,128)(2,1)S(1)}, bf16[512,192]{1,0:T(8,128)(2,1)S(1)}, bf16[512,192]{1,0:T(8,128)(2,1)S(1)}, bf16[512,192]{1,0:T(8,...) custom-call(s32[1,2]{1,0:T(1,128)S(1)} %copy-done.2, bf16[512,768]{1,0:T(8,128)(2,1)S(1)} %bitcast.183, ...), custom_call_target="tpu_custom_call" | custom-call | tf_op jit(solution)/shard_map/attention_forward/pallas_call | solution.py:225
  57.5 10.8 %all-gather = bf16[2048,192]{1,0:T(8,128)(2,1)} all-gather(bf16[512,192]{1,0:T(8,128)(2,1)S(1)} %get-tuple-element.32), channel_id=2, replica_groups=mesh['rep'=8,'fsdp'=4] {'fsdp'}, dimensions={0}, use_global_device_ids=true | all-gather | bytes 983040 | tf_op jit(solution)/shard_map/all_gather | solution.py:241
  69.7 2.3 fusion.94
  81.6 1.9 broadcast_select_fusion.2
  88.4 4.3 %all-to-all-start.1 = ((bf16[4,128,1536]{2,1,0:T(8,128)(2,1)}), bf16[4,128,1536]{2,1,0:T(8,128)(2,1)}, u32[]{:S(2)}, u32[]{:S(2)}) async-start(bf16[4,128,1536]{2,1,0:T(8,128)(2,1)} %bitcast.191), calls=%async_computation.1 | async-start | bytes 3145728 | tf_op jit(solution)/shard_map/all_to_all | solution.py:274
  92.8 2.0 convolution_convert_fusion.3
  106.3 6.7 %all-to-all-done.1 = bf16[4,128,1536]{2,1,0:T(8,128)(2,1)} async-done(((bf16[4,128,1536]{2,1,0:T(8,128)(2,1)}), bf16[4,128,1536]{2,1,0:T(8,128)(2,1)}, u32[]{:S(2)}, u32[]{:S(2)}) %all-to-all-start.1) | async-done | bytes 1572896 | tf_op jit(solution)/shard_map/all_to_all | solution.py:274
  112.9 1.8 convert_reduce_fusion
  117.2 2.3 fusion.92
  119.5 8.3 %all_gather.23 = bf16[512,768]{1,0:T(8,128)(2,1)S(1)} all-gather(bf16[128,768]{1,0:T(8,128)(2,1)S(1)} %get-tuple-element.67), channel_id=1, replica_groups=mesh['rep'=8,'fsdp'=4] {'fsdp'}, dimensions={0}, use_global_device_ids=true | all-gather | bytes 983040 | tf_op jit(solution)/shard_map/all_gather | solution.py:316
  128.8 2.9 %collective-permute-done.1 = bf16[2,2,2,96,768]{4,3,2,0,1:T(8,128)(2,1)} collective-permute-done((bf16[2,2,2,96,768]{4,3,2,0,1:T(8,128)(2,1)}, bf16[2,2,2,96,768]{4,3,2,0,1:T(8,128)(2,1)}, u32[]{:S(2)}, u32[]{:S(2)}) %collective-permute-start.1) | collective-permute-done | bytes 1179680 | tf_op jit(solution)/shard_map/ppermute | solution.py:124
  131.6 3.1 %convert_add_fusion = f32[2,2,2,96,768]{4,3,2,0,1:T(8,128)} fusion(bf16[2,2,2,96,768]{4,3,2,0,1:T(8,128)(2,1)} %collective-permute-done.1, bf16[2,1,2,2,96,768]{5,4,2,1,0,3:T(8,128)(2,1)S(1)} %copy-done.9), kind=kLoop, calls=%fused_computation.9 | loop fusion | flops 1769472 | bytes 4718592 | tf_op jit(solution)/shard_map/add | solution.py:125
  134.7 3.1 %convert_add_fusion.1 = f32[2,2,2,96,768]{4,3,2,0,1:T(8,128)} fusion(bf16[2,2,2,96,768]{4,3,2,0,1:T(8,128)(2,1)} %collective-permute-done, bf16[2,2,1,2,96,768]{5,4,2,1,0,3:T(8,128)(2,1)S(1)} %copy-done.8), kind=kLoop, calls=%fused_computation.10 | loop fusion | flops 1769472 | bytes 4718592 | tf_op jit(solution)/shard_map/add | solution.py:125
  137.8 3.9 %attention_backward.1 = (bf16[512,192]{1,0:T(8,128)(2,1)S(1)}, bf16[512,192]{1,0:T(8,128)(2,1)S(1)}, bf16[512,192]{1,0:T(8,128)(2,1)S(1)}, f32[8,1024]{1,0:T(8,128)S(1)}) custom-call(bf16[512,192]{1,0:T(8,128)(2,1)S(1)} %get-tuple-element.35.q_ref, bf16[512,192]{1,0:T(8,128)(2,1)S(1)} %get-tuple-element.36.k_ref, ...), custom_call_target="tpu_custom_call" | custom-call | flops 503316480 | bytes 12582912 | tf_op jit(solution)/shard_map/attention_backward/pallas_call | solution.py:328
  142.6 2.1 fusion.43
  144.8 2.2 fusion.44
  153.7 10.4 %collective-permute-done.8 = bf16[2,24,768]{2,1,0:T(8,128)(2,1)S(1)} collective-permute-done((bf16[2,24,768]{2,1,0:T(8,128)(2,1)S(1)}, bf16[2,24,768]{2,1,0:T(8,128)(2,1)S(1)}, u32[]{:S(2)}, u32[]{:S(2)}) %collective-permute-start.8) | collective-permute-done | bytes 73760 | tf_op jit(solution)/shard_map/ppermute | solution.py:124
  164.1 2.6 %collective-permute-start.9 = (bf16[24,768]{1,0:T(8,128)(2,1)S(1)}, bf16[24,768]{1,0:T(8,128)(2,1)S(1)}, u32[]{:S(2)}, u32[]{:S(2)}) collective-permute-start(bf16[24,768]{1,0:T(8,128)(2,1)S(1)} %fusion.67), channel_id=1, source_target_pairs={{0,16},{4,20},{8,24},{12,28},{16,0},{20,4},{24,8},{28,12},{1,17},{... | collective-permute-start | bytes 110600 | tf_op jit(solution)/shard_map/ppermute | solution.py:124
  169.0 2.1 collective-permute-start.10
  174.3 2.4 collective-permute-start.15
  177.8 4.2 %all-to-all-start.2 = ((bf16[4,144,768]{2,1,0:T(8,128)(2,1)}), bf16[4,144,768]{2,1,0:T(8,128)(2,1)}, u32[]{:S(2)}, u32[]{:S(2)}) async-start(bf16[4,144,768]{2,1,0:T(8,128)(2,1)} %fusion.36), calls=%async_computation.2 | async-start | bytes 1769472 | tf_op jit(solution)/shard_map/all_to_all | solution.py:378
  184.8 3.2 %collective-permute-start.4 = (bf16[2,2,96,576]{3,2,1,0:T(8,128)(2,1)S(1)}, bf16[2,2,96,576]{3,2,1,0:T(8,128)(2,1)S(1)}, u32[]{:S(2)}, u32[]{:S(2)}) collective-permute-start(bf16[2,2,96,576]{3,2,1,0:T(8,128)(2,1)S(1)} %dynamic-slice_bitcast_fusion), channel_id=1, source_target_pairs={{0,4},{4,0},{8,12},{12,8},{16,20},{20,16},{24,28},{28,24},{1,5},{5... | collective-permute-start | bytes 1327112 | tf_op jit(solution)/shard_map/ppermute | solution.py:124
  188.0 9.5 %collective-permute-done.15 = bf16[2,96,768]{2,1,0:T(8,128)(2,1)} collective-permute-done((bf16[2,96,768]{2,1,0:T(8,128)(2,1)}, bf16[2,96,768]{2,1,0:T(8,128)(2,1)}, u32[]{:S(2)}, u32[]{:S(2)}) %collective-permute-start.15) | collective-permute-done | bytes 294944 | tf_op jit(solution)/shard_map/ppermute | solution.py:124
  199.3 4.1 %collective-permute-start.16 = (bf16[2,96,768]{2,1,0:T(8,128)(2,1)}, bf16[2,96,768]{2,1,0:T(8,128)(2,1)S(1)}, u32[]{:S(2)}, u32[]{:S(2)}) collective-permute-start(bf16[2,96,768]{2,1,0:T(8,128)(2,1)} %fusion.45), channel_id=1, source_target_pairs={{0,0},{1,8},{2,16},{3,24},{4,1},{5,9},{6,17},{7,25},{8,2},{9,10},{... | collective-permute-start | bytes 884744 | tf_op jit(solution)/shard_map/ppermute | solution.py:151
  203.4 3.5 %collective-permute-done.14 = bf16[2,96,768]{2,1,0:T(8,128)(2,1)S(1)} collective-permute-done((bf16[2,96,768]{2,1,0:T(8,128)(2,1)S(1)}, bf16[2,96,768]{2,1,0:T(8,128)(2,1)S(1)}, u32[]{:S(2)}, u32[]{:S(2)}) %collective-permute-start.14) | collective-permute-done | bytes 294944 | tf_op jit(solution)/shard_map/ppermute | solution.py:124
  211.9 1.9 collective-permute-done.11
  214.4 8.0 %collective-permute-done.12 = f32[8,128]{1,0:T(8,128)S(1)} collective-permute-done((f32[8,128]{1,0:T(8,128)S(1)}, f32[8,128]{1,0:T(8,128)S(1)}, u32[]{:S(2)}, u32[]{:S(2)}) %collective-permute-start.12) | collective-permute-done | bytes 4128 | tf_op jit(solution)/shard_map/ppermute | solution.py:138
  222.5 3.0 %collective-permute-start.6 = (bf16[96,576]{1,0:T(8,128)(2,1)S(1)}, bf16[96,576]{1,0:T(8,128)(2,1)S(1)}, u32[]{:S(2)}, u32[]{:S(2)}) collective-permute-start(bf16[96,576]{1,0:T(8,128)(2,1)S(1)} %fusion.64), channel_id=1, source_target_pairs={{0,16},{4,20},{8,24},{12,28},{16,0},{20,4},{24,8},{28,12},{1,17},{... | collective-permute-start | bytes 331784 | tf_op jit(solution)/shard_map/ppermute | solution.py:124
  229.4 3.6 %all-to-all-start.3 = ((bf16[4,24,576]{2,1,0:T(8,128)(2,1)}), bf16[4,24,576]{2,1,0:T(8,128)(2,1)S(1)}, u32[]{:S(2)}, u32[]{:S(2)}) async-start(bf16[4,24,576]{2,1,0:T(8,128)(2,1)} %bitcast.49), calls=%async_computation.3 | async-start | bytes 245760 | tf_op jit(solution)/shard_map/all_to_all | solution.py:398
  (249 shorter events, 73.4 us)
Async XLA Ops:
  7.2 64.8 %all-gather.4.cloned.1.call-start = ((), (), s32[]{:S(2)}) async-start(), calls=%async_computation.4 | async-start | bytes 2457600 | tf_op jit(solution)/shard_map/all_gather | solution.py:199
  11.4 3.9 %copy-start.31 = (bf16[192,2]{0,1:T(2,128)(2,1)S(1)}, bf16[192,2]{0,1:T(2,128)(2,1)}, u32[]{:S(2)}) copy-start(bf16[192,2]{0,1:T(2,128)(2,1)} %param.20) | copy-start | bytes 2308
  11.4 4.4 %copy-start.11 = (bf16[128,768]{1,0:T(8,128)(2,1)S(1)}, bf16[128,768]{1,0:T(8,128)(2,1)}, u32[]{:S(2)}) copy-start(bf16[128,768]{1,0:T(8,128)(2,1)} %param.12) | copy-start | bytes 589828
  11.4 39.1 %all-to-all-start = ((bf16[4,3,192,192]{3,2,1,0:T(8,128)(2,1)}), bf16[4,3,192,192]{3,2,1,0:T(8,128)(2,1)S(1)}, u32[]{:S(2)}, u32[]{:S(2)}) async-start(bf16[4,3,192,192]{3,2,1,0:T(8,128)(2,1)} %copy.78), calls=%async_computation | async-start | bytes 2359296 | tf_op jit(solution)/shard_map/all_to_all | solution.py:212
  15.4 33.5 %copy-start.28 = (s32[1024]{0:T(1024)}, s32[1024]{0:T(1024)S(1)}, u32[]{:S(2)}) copy-start(s32[1024]{0:T(1024)S(1)} %pad.30) | copy-start | bytes 12292
  88.4 24.5 %all-to-all-start.1 = ((bf16[4,128,1536]{2,1,0:T(8,128)(2,1)}), bf16[4,128,1536]{2,1,0:T(8,128)(2,1)}, u32[]{:S(2)}, u32[]{:S(2)}) async-start(bf16[4,128,1536]{2,1,0:T(8,128)(2,1)} %bitcast.191), calls=%async_computation.1 | async-start | bytes 3145728 | tf_op jit(solution)/shard_map/all_to_all | solution.py:274
  103.0 28.6 %collective-permute-start.1 = (bf16[2,2,2,96,768]{4,3,2,0,1:T(8,128)(2,1)}, bf16[2,2,2,96,768]{4,3,2,0,1:T(8,128)(2,1)}, u32[]{:S(2)}, u32[]{:S(2)}) collective-permute-start(bf16[2,2,2,96,768]{4,3,2,0,1:T(8,128)(2,1)} %bitcast.180), channel_id=1, source_target_pairs={{0,8},{4,12},{8,0},{12,4},{16,24},{20,28},{24,16},{28,20},{1,9},{5... | collective-permute-start | bytes 3538952 | tf_op jit(solution)/shard_map/ppermute | solution.py:124
  104.6 30.2 %collective-permute-start = (bf16[2,2,2,96,768]{4,3,2,0,1:T(8,128)(2,1)}, bf16[2,2,2,96,768]{4,3,2,0,1:T(8,128)(2,1)}, u32[]{:S(2)}, u32[]{:S(2)}) collective-permute-start(bf16[2,2,2,96,768]{4,3,2,0,1:T(8,128)(2,1)} %bitcast.181), channel_id=1, source_target_pairs={{0,4},{4,0},{8,12},{12,8},{16,20},{20,16},{24,28},{28,24},{1,5},{5... | collective-permute-start | bytes 3538952 | tf_op jit(solution)/shard_map/ppermute | solution.py:124
  106.3 9.4 %copy-start.25 = (f32[768]{0:T(1024)S(1)}, f32[768]{0:T(1024)}, u32[]{:S(2)}) copy-start(f32[768]{0:T(1024)} %get-tuple-element.58) | copy-start | bytes 9220
  119.5 8.8 %copy-start.24 = (bf16[192,768]{1,0:T(8,128)(2,1)S(1)}, bf16[192,768]{1,0:T(8,128)(2,1)}, u32[]{:S(2)}) copy-start(bf16[192,768]{1,0:T(8,128)(2,1)} %param.17) | copy-start | bytes 884740
  128.3 24.0 %collective-permute-start.7 = (bf16[2,2,24,768]{3,2,0,1:T(8,128)(2,1)S(1)}, bf16[2,2,24,768]{3,2,0,1:T(8,128)(2,1)}, u32[]{:S(2)}, u32[]{:S(2)}) collective-permute-start(bf16[2,2,24,768]{3,2,0,1:T(8,128)(2,1)S(1)} %bitcast.211), channel_id=1, source_target_pairs={{0,4},{4,0},{8,12},{12,8},{16,20},{20,16},{24,28},{28,24},{1,5},{5... | collective-permute-start | bytes 442376 | tf_op jit(solution)/shard_map/ppermute | solution.py:124
  141.7 7.4 %copy-start.19 = (bf16[1,4,192,192]{3,2,0,1:T(8,128)(2,1)S(1)}, bf16[1,4,192,192]{3,2,0,1:T(8,128)(2,1)}, u32[]{:S(2)}) copy-start(bf16[1,4,192,192]{3,2,0,1:T(8,128)(2,1)} %get-tuple-element.80) | copy-start | bytes 884740
  144.8 4.7 %copy-start.18 = (bf16[1,4,192,192]{3,2,0,1:T(8,128)(2,1)S(1)}, bf16[1,4,192,192]{3,2,0,1:T(8,128)(2,1)}, u32[]{:S(2)}) copy-start(bf16[1,4,192,192]{3,2,0,1:T(8,128)(2,1)} %get-tuple-element.79) | copy-start | bytes 884740
  146.9 24.1 %collective-permute-start.3 = (bf16[2,2,96,768]{3,2,1,0:T(8,128)(2,1)}, bf16[2,2,96,768]{3,2,1,0:T(8,128)(2,1)}, u32[]{:S(2)}, u32[]{:S(2)}) collective-permute-start(bf16[2,2,96,768]{3,2,1,0:T(8,128)(2,1)} %fusion.44), channel_id=1, source_target_pairs={{0,4},{4,0},{8,12},{12,8},{16,20},{20,16},{24,28},{28,24},{1,5},{5... | collective-permute-start | bytes 1769480 | tf_op jit(solution)/shard_map/ppermute | solution.py:124
  147.3 25.0 %collective-permute-start.2 = (bf16[2,2,96,768]{3,2,1,0:T(8,128)(2,1)}, bf16[2,2,96,768]{3,2,1,0:T(8,128)(2,1)}, u32[]{:S(2)}, u32[]{:S(2)}) collective-permute-start(bf16[2,2,96,768]{3,2,1,0:T(8,128)(2,1)} %fusion.43), channel_id=1, source_target_pairs={{0,8},{4,12},{8,0},{12,4},{16,24},{20,28},{24,16},{28,20},{1,9},{5... | collective-permute-start | bytes 1769480 | tf_op jit(solution)/shard_map/ppermute | solution.py:124
  153.3 10.8 %collective-permute-start.8 = (bf16[2,24,768]{2,1,0:T(8,128)(2,1)S(1)}, bf16[2,24,768]{2,1,0:T(8,128)(2,1)S(1)}, u32[]{:S(2)}, u32[]{:S(2)}) collective-permute-start(bf16[2,24,768]{2,1,0:T(8,128)(2,1)S(1)} %fusion.65), channel_id=1, source_target_pairs={{0,8},{4,12},{8,0},{12,4},{16,24},{20,28},{24,16},{28,20},{1,9},{5... | collective-permute-start | bytes 221192 | tf_op jit(solution)/shard_map/ppermute | solution.py:124
  164.1 4.9 %collective-permute-start.9 = (bf16[24,768]{1,0:T(8,128)(2,1)S(1)}, bf16[24,768]{1,0:T(8,128)(2,1)S(1)}, u32[]{:S(2)}, u32[]{:S(2)}) collective-permute-start(bf16[24,768]{1,0:T(8,128)(2,1)S(1)} %fusion.67), channel_id=1, source_target_pairs={{0,16},{4,20},{8,24},{12,28},{16,0},{20,4},{24,8},{28,12},{1,17},{... | collective-permute-start | bytes 110600 | tf_op jit(solution)/shard_map/ppermute | solution.py:124
  166.7 4.4 %copy-start.4 = (f32[2,2,2,96,768]{4,3,2,0,1:T(8,128)S(1)}, f32[2,2,2,96,768]{4,3,2,0,1:T(8,128)}, u32[]{:S(2)}) copy-start(f32[2,2,2,96,768]{4,3,2,0,1:T(8,128)} %convert_add_fusion) | copy-start | bytes 7077892
  169.0 13.0 %collective-permute-start.10 = (bf16[24,768]{1,0:T(8,128)(2,1)S(1)}, bf16[24,768]{1,0:T(8,128)(2,1)S(1)}, u32[]{:S(2)}, u32[]{:S(2)}) collective-permute-start(bf16[24,768]{1,0:T(8,128)(2,1)S(1)} %fusion.66), channel_id=1, source_target_pairs={{0,0},{1,8},{2,16},{3,24},{4,1},{5,9},{6,17},{7,25},{8,2},{9,10},{... | collective-permute-start | bytes 110600 | tf_op jit(solution)/shard_map/ppermute | solution.py:151
  172.3 4.5 %copy-start.10 = (bf16[512,768]{1,0:T(8,128)(2,1)S(1)}, bf16[512,768]{1,0:T(8,128)(2,1)}, u32[]{:S(2)}) copy-start(bf16[512,768]{1,0:T(8,128)(2,1)} %get-tuple-element.76) | copy-start | bytes 2359300
  174.3 23.2 %collective-permute-start.15 = (bf16[2,96,768]{2,1,0:T(8,128)(2,1)}, bf16[2,96,768]{2,1,0:T(8,128)(2,1)}, u32[]{:S(2)}, u32[]{:S(2)}) collective-permute-start(bf16[2,96,768]{2,1,0:T(8,128)(2,1)} %fusion.54), channel_id=1, source_target_pairs={{0,16},{4,20},{8,24},{12,28},{16,0},{20,4},{24,8},{28,12},{1,17},{... | collective-permute-start | bytes 884744 | tf_op jit(solution)/shard_map/ppermute | solution.py:124
  177.8 30.1 %all-to-all-start.2 = ((bf16[4,144,768]{2,1,0:T(8,128)(2,1)}), bf16[4,144,768]{2,1,0:T(8,128)(2,1)}, u32[]{:S(2)}, u32[]{:S(2)}) async-start(bf16[4,144,768]{2,1,0:T(8,128)(2,1)} %fusion.36), calls=%async_computation.2 | async-start | bytes 1769472 | tf_op jit(solution)/shard_map/all_to_all | solution.py:378
  184.2 22.7 %collective-permute-start.14 = (bf16[2,96,768]{2,1,0:T(8,128)(2,1)S(1)}, bf16[2,96,768]{2,1,0:T(8,128)(2,1)S(1)}, u32[]{:S(2)}, u32[]{:S(2)}) collective-permute-start(bf16[2,96,768]{2,1,0:T(8,128)(2,1)S(1)} %fusion.53), channel_id=1, source_target_pairs={{0,16},{4,20},{8,24},{12,28},{16,0},{20,4},{24,8},{28,12},{1,17},{... | collective-permute-start | bytes 884744 | tf_op jit(solution)/shard_map/ppermute | solution.py:124
  184.8 23.0 %collective-permute-start.4 = (bf16[2,2,96,576]{3,2,1,0:T(8,128)(2,1)S(1)}, bf16[2,2,96,576]{3,2,1,0:T(8,128)(2,1)S(1)}, u32[]{:S(2)}, u32[]{:S(2)}) collective-permute-start(bf16[2,2,96,576]{3,2,1,0:T(8,128)(2,1)S(1)} %dynamic-slice_bitcast_fusion), channel_id=1, source_target_pairs={{0,4},{4,0},{8,12},{12,8},{16,20},{20,16},{24,28},{28,24},{1,5},{5... | collective-permute-start | bytes 1327112 | tf_op jit(solution)/shard_map/ppermute | solution.py:124
  199.3 35.7 %collective-permute-start.16 = (bf16[2,96,768]{2,1,0:T(8,128)(2,1)}, bf16[2,96,768]{2,1,0:T(8,128)(2,1)S(1)}, u32[]{:S(2)}, u32[]{:S(2)}) collective-permute-start(bf16[2,96,768]{2,1,0:T(8,128)(2,1)} %fusion.45), channel_id=1, source_target_pairs={{0,0},{1,8},{2,16},{3,24},{4,1},{5,9},{6,17},{7,25},{8,2},{9,10},{... | collective-permute-start | bytes 884744 | tf_op jit(solution)/shard_map/ppermute | solution.py:151
  210.0 15.5 %copy-start.17 = (f32[128,768]{1,0:T(8,128)S(1)}, f32[128,768]{1,0:T(8,128)}, u32[]{:S(2)}) copy-start(f32[128,768]{1,0:T(8,128)} %get-tuple-element.68) | copy-start | bytes 1179652
  210.1 3.6 %collective-permute-start.11 = (f32[8,128]{1,0:T(8,128)S(1)}, f32[8,128]{1,0:T(8,128)S(1)}, u32[]{:S(2)}, u32[]{:S(2)}) collective-permute-start(f32[8,128]{1,0:T(8,128)S(1)} %pad_bitcast_fusion), channel_id=1, source_target_pairs={{0,4},{4,0},{8,12},{12,8},{16,20},{20,16},{24,28},{28,24},{1,5},{5... | collective-permute-start | bytes 12296 | tf_op jit(solution)/shard_map/ppermute | solution.py:138
  210.2 12.2 %collective-permute-start.5 = (bf16[2,96,576]{2,1,0:T(8,128)(2,1)S(1)}, bf16[2,96,576]{2,1,0:T(8,128)(2,1)S(1)}, u32[]{:S(2)}, u32[]{:S(2)}) collective-permute-start(bf16[2,96,576]{2,1,0:T(8,128)(2,1)S(1)} %fusion.59), channel_id=1, source_target_pairs={{0,8},{4,12},{8,0},{12,4},{16,24},{20,28},{24,16},{28,20},{1,9},{5... | collective-permute-start | bytes 663560 | tf_op jit(solution)/shard_map/ppermute | solution.py:124
  213.8 8.6 %collective-permute-start.12 = (f32[8,128]{1,0:T(8,128)S(1)}, f32[8,128]{1,0:T(8,128)S(1)}, u32[]{:S(2)}, u32[]{:S(2)}) collective-permute-start(f32[8,128]{1,0:T(8,128)S(1)} %fusion.90), channel_id=1, source_target_pairs={{0,8},{4,12},{8,0},{12,4},{16,24},{20,28},{24,16},{28,20},{1,9},{5... | collective-permute-start | bytes 12296 | tf_op jit(solution)/shard_map/ppermute | solution.py:138
  222.4 4.9 %collective-permute-start.13 = (f32[8,128]{1,0:T(8,128)S(1)}, f32[8,128]{1,0:T(8,128)S(1)}, u32[]{:S(2)}, u32[]{:S(2)}) collective-permute-start(f32[8,128]{1,0:T(8,128)S(1)} %fusion.130), channel_id=1, source_target_pairs={{0,16},{4,20},{8,24},{12,28},{16,0},{20,4},{24,8},{28,12},{1,17},{... | collective-permute-start | bytes 12296 | tf_op jit(solution)/shard_map/ppermute | solution.py:138
  222.5 6.2 %collective-permute-start.6 = (bf16[96,576]{1,0:T(8,128)(2,1)S(1)}, bf16[96,576]{1,0:T(8,128)(2,1)S(1)}, u32[]{:S(2)}, u32[]{:S(2)}) collective-permute-start(bf16[96,576]{1,0:T(8,128)(2,1)S(1)} %fusion.64), channel_id=1, source_target_pairs={{0,16},{4,20},{8,24},{12,28},{16,0},{20,4},{24,8},{28,12},{1,17},{... | collective-permute-start | bytes 331784 | tf_op jit(solution)/shard_map/ppermute | solution.py:124
  229.4 8.2 %all-to-all-start.3 = ((bf16[4,24,576]{2,1,0:T(8,128)(2,1)}), bf16[4,24,576]{2,1,0:T(8,128)(2,1)S(1)}, u32[]{:S(2)}, u32[]{:S(2)}) async-start(bf16[4,24,576]{2,1,0:T(8,128)(2,1)} %bitcast.49), calls=%async_computation.3 | async-start | bytes 245760 | tf_op jit(solution)/shard_map/all_to_all | solution.py:398
  (32 other events, 73.5 us)
Sparse Core Ops, SparseCore 0:
  10.2 33.7 all-gather.3
